TPU v7x, 256 devices: a whole 4x4x8 slice. The times are simulated.
256 devices in a mesh: frames: 64 (over z_hi, y, x), gz: 4 (over z_lo, core).
Axes of the slice: x: 4, y: 4, z: 8 (z_hi: 4, z_lo: 2; z = z_hi * 2 + z_lo), core: 2. Of those that a mesh axis runs over, the one named last changes fastest.
Arguments:
- recording: bfloat16 [128, 32, 1024, 128], P('frames', 'gz'), may hold values from -6 to 6
- group_ids: int32 [128], replicated, may hold values from 0 to 15, never falling along the last dimension, each value on 1 to 16 neighbouring positions
- shifts: float32 [16, 2], replicated, may hold values from -0.9 to 0.9
- fir_taps: float32 [31], replicated, may hold values from 0.05 to 1
Outputs:
- correlation: float32 [32, 1024, 128], P('gz', 'frames')
Inputs may be any that keep to these rules, and one draw needn't show every extreme that they name: `group_ids`: frames of one group are consecutive: ids never fall along the frames, and every id occurs.
All inputs are finite; a program needn't handle non-finite values.
Results may differ from a plain program's by a relative error of at most 0.0033.
Values may be sent and summed in bfloat16 or wider, within the bound.
No kernel may reach another device: no remote copies, remote signals or barrier semaphores. Data moves between devices by JAX's collectives and lax.ppermute only.
A program may use at most 128 MiB of HBM per device.

v0:
```python
import functools

import jax
import jax.numpy as jnp
import numpy as np
from jax import lax
from jax.experimental import pallas as pl
from jax.experimental.pallas import tpu as pltpu
from jax.sharding import PartitionSpec as P

RADIUS = 3
EPSILON = 1e-05
SIGMA_XY = 1.5
SIGMA_Z = 1.0
HALF = 4
VMEM = 56 * 1024 * 1024


def gaussian(sigma):
    offsets = np.arange(-RADIUS, RADIUS + 1).astype(np.float32)
    values = np.exp(-offsets * offsets / np.float32(2.0 * sigma * sigma)).astype(np.float32)
    return (values / values.sum(dtype=np.float32)).astype(np.float32)


KERNEL_X = gaussian(SIGMA_XY).astype(jnp.bfloat16).astype(np.float32)
KERNEL_Y = gaussian(SIGMA_XY)
KERNEL_Z = gaussian(SIGMA_Z)
CENTER = float(np.float32(np.float32(KERNEL_Z[RADIUS] * KERNEL_Y[RADIUS]) * KERNEL_X[RADIUS]))


COST = pl.CostEstimate(flops=1, bytes_accessed=1, transcendentals=0)


def params(*semantics):
    return pltpu.CompilerParams(dimension_semantics=semantics, vmem_limit_bytes=VMEM)


def register_kernel(first_ref, groups_ref, shifts_ref, x_ref, out_ref, aligned):
    frame = pl.program_id(0)
    planes, rows, width = x_ref.shape[1:]
    tile = rows // out_ref.shape[0]
    group = groups_ref[first_ref[0] + frame]
    shift_y, shift_x = shifts_ref[group, 0], shifts_ref[group, 1]
    lane = lax.broadcasted_iota(jnp.int32, (8, width), 1)
    upper = lax.broadcasted_iota(jnp.int32, (8, width), 0) < HALF
    back = shift_x > 0.0
    edge = jnp.where(back, 0, width - 1)
    roll = jnp.where(back, 1, width - 1)
    side_x = jnp.where(lane == edge, 0.0, jnp.abs(shift_x))[None]
    here_x = 1.0 - jnp.abs(shift_x)
    zeros = jnp.zeros((8, width), jnp.float32)
    step = min(128, rows)
    for plane in range(planes):
        aligned[plane, 0:8] = zeros
        aligned[plane, rows + 8 : rows + 16] = zeros
        for start in range(0, rows, step):
            values = x_ref[0, plane, start : start + step].astype(jnp.float32)
            moved = pltpu.roll(values, roll, 1).reshape(step // 8, 8, width)
            mixed = here_x * values.reshape(step // 8, 8, width) + side_x * moved
            aligned[plane, 8 + start : 8 + start + step] = mixed.reshape(step, width)
    here_y, side_y = 1.0 - jnp.abs(shift_y), jnp.abs(shift_y)

    def finish(offset):
        def unit(plane, row):
            here = aligned[plane, 8 + row : 16 + row]
            beside = aligned[plane, 8 + offset + row : 16 + offset + row]
            return here_y * here + side_y * beside

        before = [unit(plane, -HALF) for plane in range(planes)]
        for t in range(rows // tile):
            middle, ends = [], []
            for plane in range(planes):
                middle.append(unit(plane, t * tile + HALF))
                after = unit(plane, t * tile + tile - HALF)
                ends.append(jnp.where(upper, after, before[plane]))
                before[plane] = after
            out_ref[t, 0, 0] = jnp.concatenate(ends, axis=0).astype(out_ref.dtype)
            out_ref[t, 0, 1] = jnp.concatenate(middle, axis=0).astype(out_ref.dtype)

    pl.when(shift_y > 0.0)(lambda: finish(-1))
    pl.when(shift_y <= 0.0)(lambda: finish(1))


def register(recording, group_ids, shifts, first, tiles):
    frames, planes, rows, width = recording.shape
    smem = pl.BlockSpec(memory_space=pltpu.SMEM)
    return pl.pallas_call(
        register_kernel,
        grid=(frames, planes // 2),
        in_specs=[smem, smem, smem, pl.BlockSpec((1, 2, rows, width), lambda f, j: (f, j, 0, 0))],
        out_specs=pl.BlockSpec((tiles, 1, 2, 16, width), lambda f, j: (0, f, 0, j, 0)),
        out_shape=jax.ShapeDtypeStruct((tiles, frames, 2, planes * 8, width), recording.dtype),
        scratch_shapes=[pltpu.VMEM((2, rows + 16, width), jnp.float32)],
        cost_estimate=COST,
        compiler_params=params("arbitrary", "arbitrary"),
        name="register",
    )(first, group_ids, shifts, recording)


def filter_kernel(part, taps_ref, x_ref, out_ref, low_ref, high_ref, *rest):
    matrix, rows = rest[-2:]
    frames, _, tile, width = x_ref.shape
    planes = out_ref.shape[0]
    taps = taps_ref.shape[0]
    reach = (taps - 1) // 2
    step = pl.program_id(0)

    @pl.when(step == 0)
    def _():
        t = lax.broadcasted_iota(jnp.int32, (frames, frames), 0)
        u = lax.broadcasted_iota(jnp.int32, (frames, frames), 1)
        distance = u - t + reach
        band = jnp.zeros((frames, frames), jnp.float32)
        for k in range(taps):
            band = jnp.where(distance == k, taps_ref[k], band)
        matrix[...] = (band / jnp.sum(band, axis=1, keepdims=True)).astype(matrix.dtype)

    rows[...] = x_ref[...].astype(jnp.float32).reshape(frames * tile, width)
    weights = matrix[...]
    for cell in range(tile):
        values = rows[pl.ds(cell, frames, stride=tile), :]
        baseline = jnp.dot(weights, values.astype(jnp.bfloat16), preferred_element_type=jnp.float32)
        detrended = values - baseline
        average = jnp.sum(detrended, axis=0, keepdims=True) * (1.0 / frames)
        centred = detrended - average
        power = jnp.sum(centred * centred, axis=0, keepdims=True) * (1.0 / frames)
        out_ref[cell // 8, cell % 8] = (centred * lax.rsqrt(power + EPSILON)).astype(out_ref.dtype)
    for p in range(planes):
        plane = step * planes + p

        @pl.when(plane < RADIUS)
        def _():
            low_ref[plane] = out_ref[p]

        first = pl.num_programs(0) * planes - RADIUS

        @pl.when(plane >= first)
        def _():
            high_ref[plane - first] = out_ref[p]

        if part == 0:
            rest[0][p] = out_ref[p, HALF - RADIUS : HALF]
            rest[1][p] = out_ref[p, HALF : HALF + RADIUS]


def filter_cells(registered, fir_taps, part):
    frames, _, cells, width = registered.shape
    planes = cells // 8

    def shape(*size):
        return jax.ShapeDtypeStruct((*size, frames, width), registered.dtype)

    slab = pl.BlockSpec((RADIUS, 8, frames, width), lambda z: (0, 0, 0, 0))
    rows = pl.BlockSpec((2, RADIUS, frames, width), lambda z: (z, 0, 0, 0))
    return pl.pallas_call(
        functools.partial(filter_kernel, part),
        grid=(planes // 2,),
        in_specs=[
            pl.BlockSpec(memory_space=pltpu.SMEM),
            pl.BlockSpec((frames, 1, 16, width), lambda z: (0, part, z, 0)),
        ],
        out_specs=[pl.BlockSpec((2, 8, frames, width), lambda z: (z, 0, 0, 0)), slab, slab] + [rows, rows][: 2 - 2 * part],
        out_shape=[shape(planes, 8), shape(RADIUS, 8), shape(RADIUS, 8)] + [shape(planes, RADIUS)] * (2 - 2 * part),
        scratch_shapes=[pltpu.VMEM((frames, frames), jnp.bfloat16), pltpu.VMEM((frames * 16, width), jnp.float32)],
        cost_estimate=COST,
        compiler_params=params("arbitrary"),
        name="filter",
    )(fir_taps, registered)


def pair_sums(parts, taps):
    total = taps[RADIUS] * parts[RADIUS]
    for k in range(RADIUS):
        total = total + taps[k] * (parts[k] + parts[2 * RADIUS - k])
    return total


TAPS_Y = [float(v) for v in KERNEL_Y]
TAPS_Z = [float(v) for v in KERNEL_Z]
WINDOW = 2 * RADIUS + 1
SCRATCH = 16


def smooth_z(current, target):
    planes = target.shape[0]
    for start in range(0, current.shape[1], 16):
        parts = [current[z, start : start + 16].astype(jnp.float32) for z in range(planes + 2 * RADIUS)]
        for z in range(planes):
            target[z, start : start + 16] = pair_sums(parts[z : z + WINDOW], TAPS_Z)


def band_of(matrix):
    width = matrix.shape[0]
    distance = lax.broadcasted_iota(jnp.int32, (width, width), 1) - lax.broadcasted_iota(
        jnp.int32, (width, width), 0
    )
    band = jnp.zeros((width, width), jnp.float32)
    for k in range(WINDOW):
        band = jnp.where(distance == k - RADIUS, float(KERNEL_X[k]), band)
    matrix[...] = band.astype(matrix.dtype)


def row_of_image(mixed, values_of, matrix, out_ref, y):
    for z in range(mixed.shape[0]):
        smoothed = jnp.dot(mixed[z], matrix[...], preferred_element_type=jnp.float32)
        values = values_of(z).astype(jnp.float32)
        frames = values.shape[0]
        total = jnp.sum(values * (smoothed - CENTER * values), axis=0, keepdims=True)
        out_ref[z, pl.ds(y, 1), :] = total * (1.0 / (frames * (1.0 - CENTER)))


def inner_kernel(ends, middle, low_ends, high_ends, low_middle, high_middle, out_ref, part_ref, *scratch):
    current, ring, mixed, values, matrix = scratch
    planes, tile = out_ref.shape[0], out_ref.shape[1]
    frames = current.shape[1]
    band_of(matrix)
    for row in range(RADIUS):
        ring[row] = jnp.zeros(ring.shape[1:], ring.dtype)

    def take(y):
        inside = (y >= HALF) & (y < tile - HALF)
        row = jnp.where(inside, y - HALF, jnp.where(y < HALF, y + HALF, y - (tile - HALF)))

        def fill(low, own, high):
            for k in range(RADIUS):
                current[k] = low[k, row]
                current[RADIUS + planes + k] = high[k, row]
            for z in range(planes):
                current[RADIUS + z] = own[z, row]

        pl.when(inside)(lambda: fill(low_middle, middle, high_middle))
        pl.when(jnp.logical_not(inside))(lambda: fill(low_ends, ends, high_ends))
        smooth_z(current, ring.at[lax.rem(y + RADIUS, WINDOW)])

    def rows_of(y, z, start):
        return pair_sums([ring[lax.rem(y + k, WINDOW), z, start : start + 32] for k in range(WINDOW)], TAPS_Y)

    def give_part(y, at):
        for z in range(planes):
            for start in range(0, frames, 32):
                part_ref[at, z, start : start + 32] = rows_of(y, z, start)

    def give(y):
        inside = (y >= HALF) & (y < tile - HALF)
        row = jnp.where(inside, y - HALF, jnp.where(y < HALF, y + HALF, y - (tile - HALF)))

        def fill(own):
            for z in range(planes):
                values[z] = own[z, row]

        pl.when(inside)(lambda: fill(middle))
        pl.when(jnp.logical_not(inside))(lambda: fill(ends))
        for z in range(planes):
            for start in range(0, frames, 32):
                mixed[z, start : start + 32] = rows_of(y, z, start).astype(mixed.dtype)
        row_of_image(mixed, lambda z: values[z], matrix, out_ref, y)

    pl.loop(0, RADIUS)(take)

    @pl.loop(RADIUS, 2 * RADIUS)
    def _(y):
        take(y)
        give_part(y - RADIUS, y - RADIUS)

    @pl.loop(2 * RADIUS, tile)
    def _(y):
        take(y)
        give(y - RADIUS)

    @pl.loop(tile, tile + RADIUS)
    def _(y):
        slot = lax.rem(y + RADIUS, WINDOW)
        ring[slot] = jnp.zeros(ring.shape[1:], ring.dtype)
        give_part(y - RADIUS, y - tile + RADIUS)


def outer_kernel(ends, part, image, *refs):
    sides, (out_ref, current, halo, mixed, matrix) = refs[:-5], refs[-5:]
    planes, tile = out_ref.shape[0], out_ref.shape[1]
    frames = current.shape[1]
    band_of(matrix)
    out_ref[...] = image[...]

    def side(low, own, high, first, upper):
        @pl.loop(0, RADIUS)
        def _(k):
            for j in range(RADIUS):
                current[j] = low[j, first + k]
                current[RADIUS + planes + j] = high[j, first + k]
            for z in range(planes):
                current[RADIUS + z] = own[z, k]
            smooth_z(current, halo.at[k])

        for n in range(RADIUS):
            y = tile - RADIUS + n if upper else n
            taps = [((tile + k if upper else k - RADIUS) - y + RADIUS, k) for k in range(RADIUS)]
            taps = [(TAPS_Y[at], k) for at, k in taps if 0 <= at < WINDOW]
            for z in range(planes):
                for start in range(0, frames, 32):
                    total = part[n + RADIUS * upper, z, start : start + 32]
                    for tap, k in taps:
                        total = total + tap * halo[k, z, start : start + 32]
                    mixed[z, start : start + 32] = total.astype(mixed.dtype)
            row = y - (tile - HALF) if upper else y + HALF
            row_of_image(mixed, lambda z: ends[z, row], matrix, out_ref, y)

    below, above, low_corners, high_corners = sides
    side(low_corners, below, high_corners, 0, 0)
    side(low_corners, above, high_corners, RADIUS, 1)


def inner(ends, middle, slabs_ends, slabs_middle, tile):
    planes, _, frames, width = ends.shape
    vmem = pl.BlockSpec(memory_space=pltpu.VMEM)
    return pl.pallas_call(
        inner_kernel,
        in_specs=[vmem] * 6,
        out_specs=[vmem] * 2,
        out_shape=[
            jax.ShapeDtypeStruct((planes, tile, width), jnp.float32),
            jax.ShapeDtypeStruct((2 * RADIUS, planes, frames, width), jnp.float32),
        ],
        scratch_shapes=[
            pltpu.VMEM((planes + 2 * RADIUS, frames, width), jnp.bfloat16),
            pltpu.VMEM((WINDOW, planes, frames, width), jnp.float32),
            pltpu.VMEM((planes, frames, width), jnp.bfloat16),
            pltpu.VMEM((planes, frames, width), jnp.bfloat16),
            pltpu.VMEM((width, width), jnp.bfloat16),
        ],
        cost_estimate=COST,
        compiler_params=pltpu.CompilerParams(vmem_limit_bytes=SCRATCH * 2**21),
        name="inner",
    )(ends, middle, *slabs_ends, *slabs_middle)


def outer(ends, part, image, below, above, corners):
    planes, _, frames, width = ends.shape
    vmem = pl.BlockSpec(memory_space=pltpu.VMEM)
    return pl.pallas_call(
        outer_kernel,
        in_specs=[vmem] * 7,
        out_specs=vmem,
        out_shape=jax.ShapeDtypeStruct(image.shape, jnp.float32),
        scratch_shapes=[
            pltpu.VMEM((planes + 2 * RADIUS, frames, width), jnp.bfloat16),
            pltpu.VMEM((RADIUS, planes, frames, width), jnp.float32),
            pltpu.VMEM((planes, frames, width), jnp.bfloat16),
            pltpu.VMEM((width, width), jnp.bfloat16),
        ],
        cost_estimate=COST,
        compiler_params=pltpu.CompilerParams(vmem_limit_bytes=SCRATCH * 2**21),
        name="outer",
    )(ends, part, image, below, above, *corners)


def body(recording, group_ids, shifts, fir_taps):
    planes, rows = recording.shape[1], recording.shape[2]
    tiles, slabs = lax.axis_size("frames"), lax.axis_size("gz")
    tile = rows // tiles
    first = (lax.axis_index("frames") * recording.shape[0]).reshape(1)

    def shift(array, axis, by):
        count = lax.axis_size(axis)
        return lax.ppermute(array, axis, [(i, i + by) for i in range(count) if 0 <= i + by < count])

    sent = register(recording, group_ids, shifts, first, tiles)
    arrived = lax.all_to_all(sent, "frames", 0, 0)
    arrived = arrived.reshape(-1, *arrived.shape[2:])
    ends, low_ends, high_ends, up, down = filter_cells(arrived, fir_taps, 0)
    below, above = shift(up, "frames", 1), shift(down, "frames", -1)
    slabs_ends = [shift(high_ends, "gz", 1), shift(low_ends, "gz", -1)]
    middle, low_middle, high_middle = filter_cells(arrived, fir_taps, 1)
    slabs_middle = [shift(high_middle, "gz", 1), shift(low_middle, "gz", -1)]
    image, part = inner(ends, middle, slabs_ends, slabs_middle, tile)
    part, below, above = lax.optimization_barrier((part, below, above))
    corners = []
    for at, by in ((planes - RADIUS, 1), (0, -1)):
        both = jnp.concatenate([below[at : at + RADIUS], above[at : at + RADIUS]], axis=1)
        corners.append(shift(both, "gz", by))
    return outer(ends, part, image, below, above, corners)


def solution(mesh):
    placed = (P("frames", "gz", None, None), P(), P(), P())
    return jax.shard_map(
        body, mesh=mesh, in_specs=placed, out_specs=P("gz", "frames", None), check_vma=False
    )
```

profile of v0, /device:TPU:65, one launch (start us, length us, event | category | flops | bytes accessed | tf_op | source)
XLA Modules:
  0.0 208.1 jit_solution(5400360382851337661)
XLA Ops:
  0.0 1.4 copy.5.shifts_ref
  1.4 8.0 %register.1 = bf16[64,2,2,64,128]{4,3,2,1,0:T(8,128)(2,1)} custom-call(s32[1]{0:T(128)} %bitcast.first_ref, s32[128]{0:T(128)} %groups_ref.1, f32[16,2]{1,0:T(8,128)} %copy.5.shifts_ref, bf16[2,8,1024,128]{3,2,1,0:T(8,128)(2,1)} %x_ref.1), custom_call_target="tpu_custom_call" | custom-call | flops 1 | bytes 1 | tf_op jit(solution)/shard_map/register/pallas_call | solution.py:87
  9.3 103.6 %all_to_all.5 = bf16[64,2,2,64,128]{4,3,2,1,0:T(8,128)(2,1)} all-to-all(bf16[64,2,2,64,128]{4,3,2,1,0:T(8,128)(2,1)} %register.1), channel_id=1, replica_groups=mesh['frames'=64,'gz'=4] {'frames'}, dimensions={0} | all-to-all | bytes 8388608 | tf_op jit(solution)/shard_map/all_to_all | solution.py:367
  112.9 6.4 %filter.3 = (bf16[8,8,128,128]{3,2,1,0:T(8,128)(2,1)}, bf16[3,8,128,128]{3,2,1,0:T(8,128)(2,1)}, bf16[3,8,128,128]{3,2,1,0:T(8,128)(2,1)}) custom-call(f32[31]{0:T(128)} %taps_ref.3, bf16[128,2,64,128]{3,2,1,0:T(8,128)(2,1)} %bitcast.2), custom_call_target="tpu_custom_call" | custom-call | flops 1 | bytes 1 | tf_op jit(solution)/shard_map/filter/pallas_call | solution.py:155
  119.3 0.0 copy-start.2
  119.3 0.0 copy-start.1
  119.3 9.7 %collective-permute-start.2 = (bf16[3,8,128,128]{3,2,1,0:T(8,128)(2,1)}, bf16[3,8,128,128]{3,2,1,0:T(8,128)(2,1)S(1)}, u32[]{:S(2)}, u32[]{:S(2)}) collective-permute-start(bf16[3,8,128,128]{3,2,1,0:T(8,128)(2,1)} %get-tuple-element.22), channel_id=1, source_target_pairs={{0,1},{1,2},{2,3},{4,5},{5,6},{6,7},{8,9},{9,10},{10,11},{12,13},{... | collective-permute-start | bytes 2359304 | tf_op jit(solution)/shard_map/ppermute | solution.py:364
  129.1 6.9 %filter.2 = (bf16[8,8,128,128]{3,2,1,0:T(8,128)(2,1)}, bf16[3,8,128,128]{3,2,1,0:T(8,128)(2,1)}, bf16[3,8,128,128]{3,2,1,0:T(8,128)(2,1)}, bf16[8,3,128,128]{3,2,1,0:T(8,128)(2,1)}, bf16[8,3,128,128]{3,2,1,0:T(8,128)(2,1)}) custom-call(f32[31]{0:T(128)} %taps_ref.3, bf16[128,2,64,128]{3,2,1,0:T(8,128)(2,1)} %bitcast.3), custom_call_target="tpu_custom_call" | custom-call | flops 1 | bytes 1 | tf_op jit(solution)/shard_map/filter/pallas_call | solution.py:155
  135.9 0.0 copy-done.2
  135.9 1.9 collective-permute-start.3
  137.9 3.6 %collective-permute-start = (bf16[3,8,128,128]{3,2,1,0:T(8,128)(2,1)}, bf16[3,8,128,128]{3,2,1,0:T(8,128)(2,1)S(1)}, u32[]{:S(2)}, u32[]{:S(2)}) collective-permute-start(bf16[3,8,128,128]{3,2,1,0:T(8,128)(2,1)} %get-tuple-element.20), channel_id=1, source_target_pairs={{0,1},{1,2},{2,3},{4,5},{5,6},{6,7},{8,9},{9,10},{10,11},{12,13},{... | collective-permute-start | bytes 2359304 | tf_op jit(solution)/shard_map/ppermute | solution.py:364
  141.5 1.9 collective-permute-start.1
  143.4 2.1 collective-permute-start.4
  145.5 0.0 collective-permute-done.2.low_middle
  145.5 8.3 %collective-permute-start.5 = (bf16[8,3,128,128]{3,2,1,0:T(8,128)(2,1)}, bf16[8,3,128,128]{3,2,1,0:T(8,128)(2,1)S(1)}, u32[]{:S(2)}, u32[]{:S(2)}) collective-permute-start(bf16[8,3,128,128]{3,2,1,0:T(8,128)(2,1)} %get-tuple-element.26), channel_id=1, source_target_pairs={{4,0},{8,4},{12,8},{16,12},{20,16},{24,20},{28,24},{32,28},{36,32}... | collective-permute-start | bytes 2359304 | tf_op jit(solution)/shard_map/ppermute | solution.py:364
  153.9 0.0 collective-permute-done.3.high_middle
  153.9 0.0 collective-permute-done.low_ends
  153.9 12.3 %collective-permute-done.1.high_ends = bf16[3,8,128,128]{3,2,1,0:T(8,128)(2,1)S(1)} collective-permute-done((bf16[3,8,128,128]{3,2,1,0:T(8,128)(2,1)}, bf16[3,8,128,128]{3,2,1,0:T(8,128)(2,1)S(1)}, u32[]{:S(2)}, u32[]{:S(2)}) %collective-permute-start.1) | collective-permute-done | bytes 786464 | tf_op jit(solution)/shard_map/ppermute | solution.py:364
  166.2 0.0 copy-done.1
  166.2 0.0 copy-start
  166.2 1.6 copy-done
  167.8 9.8 %inner.1 = (f32[8,16,128]{2,1,0:T(8,128)S(1)}, f32[6,8,128,128]{3,2,1,0:T(8,128)S(1)}) custom-call(bf16[8,8,128,128]{3,2,1,0:T(8,128)(2,1)S(1)} %copy-done, bf16[8,8,128,128]{3,2,1,0:T(8,128)(2,1)S(1)} %copy-done.1, bf16[3,8,128,128]{3,2,1,0:T(8,128)(2,1)S(1)} %collective-permute-done.low_ends, ...), custom_call_target="tpu_custom_call" | custom-call | flops 1 | bytes 1 | tf_op jit(solution)/shard_map/inner/pallas_call | solution.py:315
  177.6 0.0 collective-permute-done.4.refs_0_
  177.6 8.2 %collective-permute-done.5.refs_1_ = bf16[8,3,128,128]{3,2,1,0:T(8,128)(2,1)S(1)} collective-permute-done((bf16[8,3,128,128]{3,2,1,0:T(8,128)(2,1)}, bf16[8,3,128,128]{3,2,1,0:T(8,128)(2,1)S(1)}, u32[]{:S(2)}, u32[]{:S(2)}) %collective-permute-start.5) | collective-permute-done | bytes 786464 | tf_op jit(solution)/shard_map/ppermute | solution.py:364
  185.7 0.1 fusion
  185.9 0.1 pad_maximum_fusion
  185.9 7.5 %collective-permute-start.6 = (bf16[3,6,128,128]{3,2,1,0:T(8,128)(2,1)S(1)}, bf16[3,6,128,128]{3,2,1,0:T(8,128)(2,1)S(1)}, u32[]{:S(2)}, u32[]{:S(2)}) collective-permute-start(bf16[3,6,128,128]{3,2,1,0:T(8,128)(2,1)S(1)} %pad_maximum_fusion), channel_id=1, source_target_pairs={{0,1},{1,2},{2,3},{4,5},{5,6},{6,7},{8,9},{9,10},{10,11},{12,13},{... | collective-permute-start | bytes 1769480 | tf_op jit(solution)/shard_map/ppermute | solution.py:364
  193.5 0.1 pad_maximum_fusion.1
  193.5 1.9 collective-permute-start.7
  195.5 4.8 %collective-permute-done.6.refs_2_ = bf16[3,6,128,128]{3,2,1,0:T(8,128)(2,1)S(1)} collective-permute-done((bf16[3,6,128,128]{3,2,1,0:T(8,128)(2,1)S(1)}, bf16[3,6,128,128]{3,2,1,0:T(8,128)(2,1)S(1)}, u32[]{:S(2)}, u32[]{:S(2)}) %collective-permute-start.6) | collective-permute-done | bytes 589856 | tf_op jit(solution)/shard_map/ppermute | solution.py:364
  200.3 4.5 %collective-permute-done.7.refs_3_ = bf16[3,6,128,128]{3,2,1,0:T(8,128)(2,1)S(1)} collective-permute-done((bf16[3,6,128,128]{3,2,1,0:T(8,128)(2,1)S(1)}, bf16[3,6,128,128]{3,2,1,0:T(8,128)(2,1)S(1)}, u32[]{:S(2)}, u32[]{:S(2)}) %collective-permute-start.7) | collective-permute-done | bytes 589856 | tf_op jit(solution)/shard_map/ppermute | solution.py:364
  204.7 3.4 %outer.1 = f32[8,16,128]{2,1,0:T(8,128)} custom-call(bf16[8,8,128,128]{3,2,1,0:T(8,128)(2,1)S(1)} %copy-done, f32[6,8,128,128]{3,2,1,0:T(8,128)S(1)} %get-tuple-element.27.part, f32[8,16,128]{2,1,0:T(8,128)S(1)} %get-tuple-element.28.image, bf16[8,3,128,128]{3,2,1,0:T(8,128)(2,1)S(1)} %collective-permute-done.4.refs_0_, ...), custom_call_target="tpu_custom_call" | custom-call | flops 1 | bytes 1 | tf_op jit(solution)/shard_map/outer/pallas_call | solution.py:339
Async XLA Ops:
  119.3 16.6 %copy-start.2 = (bf16[3,8,128,128]{3,2,1,0:T(8,128)(2,1)S(1)}, bf16[3,8,128,128]{3,2,1,0:T(8,128)(2,1)}, u32[]{:S(2)}) copy-start(bf16[3,8,128,128]{3,2,1,0:T(8,128)(2,1)} %get-tuple-element.23) | copy-start | bytes 2359300
  119.3 46.8 %copy-start.1 = (bf16[8,8,128,128]{3,2,1,0:T(8,128)(2,1)S(1)}, bf16[8,8,128,128]{3,2,1,0:T(8,128)(2,1)}, u32[]{:S(2)}) copy-start(bf16[8,8,128,128]{3,2,1,0:T(8,128)(2,1)} %get-tuple-element.19.middle) | copy-start | bytes 6291460
  119.3 26.2 %collective-permute-start.2 = (bf16[3,8,128,128]{3,2,1,0:T(8,128)(2,1)}, bf16[3,8,128,128]{3,2,1,0:T(8,128)(2,1)S(1)}, u32[]{:S(2)}, u32[]{:S(2)}) collective-permute-start(bf16[3,8,128,128]{3,2,1,0:T(8,128)(2,1)} %get-tuple-element.22), channel_id=1, source_target_pairs={{0,1},{1,2},{2,3},{4,5},{5,6},{6,7},{8,9},{9,10},{10,11},{12,13},{... | collective-permute-start | bytes 2359304 | tf_op jit(solution)/shard_map/ppermute | solution.py:364
  135.9 17.9 %collective-permute-start.3 = (bf16[3,8,128,128]{3,2,1,0:T(8,128)(2,1)S(1)}, bf16[3,8,128,128]{3,2,1,0:T(8,128)(2,1)S(1)}, u32[]{:S(2)}, u32[]{:S(2)}) collective-permute-start(bf16[3,8,128,128]{3,2,1,0:T(8,128)(2,1)S(1)} %copy-done.2), channel_id=1, source_target_pairs={{1,0},{2,1},{3,2},{5,4},{6,5},{7,6},{9,8},{10,9},{11,10},{13,12},{... | collective-permute-start | bytes 2359304 | tf_op jit(solution)/shard_map/ppermute | solution.py:364
  137.9 16.0 %collective-permute-start = (bf16[3,8,128,128]{3,2,1,0:T(8,128)(2,1)}, bf16[3,8,128,128]{3,2,1,0:T(8,128)(2,1)S(1)}, u32[]{:S(2)}, u32[]{:S(2)}) collective-permute-start(bf16[3,8,128,128]{3,2,1,0:T(8,128)(2,1)} %get-tuple-element.20), channel_id=1, source_target_pairs={{0,1},{1,2},{2,3},{4,5},{5,6},{6,7},{8,9},{9,10},{10,11},{12,13},{... | collective-permute-start | bytes 2359304 | tf_op jit(solution)/shard_map/ppermute | solution.py:364
  141.5 24.6 %collective-permute-start.1 = (bf16[3,8,128,128]{3,2,1,0:T(8,128)(2,1)}, bf16[3,8,128,128]{3,2,1,0:T(8,128)(2,1)S(1)}, u32[]{:S(2)}, u32[]{:S(2)}) collective-permute-start(bf16[3,8,128,128]{3,2,1,0:T(8,128)(2,1)} %get-tuple-element.21), channel_id=1, source_target_pairs={{1,0},{2,1},{3,2},{5,4},{6,5},{7,6},{9,8},{10,9},{11,10},{13,12},{... | collective-permute-start | bytes 2359304 | tf_op jit(solution)/shard_map/ppermute | solution.py:364
  143.4 34.1 %collective-permute-start.4 = (bf16[8,3,128,128]{3,2,1,0:T(8,128)(2,1)}, bf16[8,3,128,128]{3,2,1,0:T(8,128)(2,1)S(1)}, u32[]{:S(2)}, u32[]{:S(2)}) collective-permute-start(bf16[8,3,128,128]{3,2,1,0:T(8,128)(2,1)} %get-tuple-element.25), channel_id=1, source_target_pairs={{0,4},{4,8},{8,12},{12,16},{16,20},{20,24},{24,28},{28,32},{32,36}... | collective-permute-start | bytes 2359304 | tf_op jit(solution)/shard_map/ppermute | solution.py:364
  145.5 40.2 %collective-permute-start.5 = (bf16[8,3,128,128]{3,2,1,0:T(8,128)(2,1)}, bf16[8,3,128,128]{3,2,1,0:T(8,128)(2,1)S(1)}, u32[]{:S(2)}, u32[]{:S(2)}) collective-permute-start(bf16[8,3,128,128]{3,2,1,0:T(8,128)(2,1)} %get-tuple-element.26), channel_id=1, source_target_pairs={{4,0},{8,4},{12,8},{16,12},{20,16},{24,20},{28,24},{32,28},{36,32}... | collective-permute-start | bytes 2359304 | tf_op jit(solution)/shard_map/ppermute | solution.py:364
  166.2 1.6 copy-start
  185.9 14.4 %collective-permute-start.6 = (bf16[3,6,128,128]{3,2,1,0:T(8,128)(2,1)S(1)}, bf16[3,6,128,128]{3,2,1,0:T(8,128)(2,1)S(1)}, u32[]{:S(2)}, u32[]{:S(2)}) collective-permute-start(bf16[3,6,128,128]{3,2,1,0:T(8,128)(2,1)S(1)} %pad_maximum_fusion), channel_id=1, source_target_pairs={{0,1},{1,2},{2,3},{4,5},{5,6},{6,7},{8,9},{9,10},{10,11},{12,13},{... | collective-permute-start | bytes 1769480 | tf_op jit(solution)/shard_map/ppermute | solution.py:364
  193.5 11.2 %collective-permute-start.7 = (bf16[3,6,128,128]{3,2,1,0:T(8,128)(2,1)S(1)}, bf16[3,6,128,128]{3,2,1,0:T(8,128)(2,1)S(1)}, u32[]{:S(2)}, u32[]{:S(2)}) collective-permute-start(bf16[3,6,128,128]{3,2,1,0:T(8,128)(2,1)S(1)} %pad_maximum_fusion.1), channel_id=1, source_target_pairs={{1,0},{2,1},{3,2},{5,4},{6,5},{7,6},{9,8},{10,9},{11,10},{13,12},{... | collective-permute-start | bytes 1769480 | tf_op jit(solution)/shard_map/ppermute | solution.py:364
where the time goes:
time: 212 us; the launch traced here: 208 us
  blocking collectives  104 us (49%)
  starting transfers between devices  37.1 us (18%)
  Pallas kernels  34.5 us (16%)
  waiting for transfers between devices  29.7 us (14%)
  local copies, waits for them, and re-layouts  3.06 us (1%)
    all_to_all x1, blocking collectives, body(): arrived = lax.all_to_all(sent, 'frames', 0, 0)  104 us
    ppermute x8, starting transfers between devices, shift(): lax.ppermute(array, axis, [(i, i + by) for i in range(count) if 0 <= i +...  37.1 us
    ppermute x8, waiting for transfers between devices, shift(): lax.ppermute(array, axis, [(i, i + by) for i in range(count) if 0 <= i +...  29.7 us
    pallas_call x2, Pallas kernels, filter_cells(): pl.pallas_call(functools.partial(filter_kernel, part), grid=(planes // 2,...  13.3 us
    pallas_call x1, Pallas kernels, inner(): pl.pallas_call(inner_kernel, in_specs=[vmem] * 6, out_specs=[vmem] * 2, o...  9.81 us
    pallas_call x1, Pallas kernels, register(): pl.pallas_call(register_kernel, grid=(frames, planes // 2), in_specs=[sme...  7.97 us
  transfers between devices with their start and end apart: 8, of which 4 were waited for; matrix products, arithmetic and copies ran while one was open for 0% of the time, Pallas kernels for 8%

commit v1 on v0

--- a/solution.py
+++ b/solution.py
@@ -13,7 +13,9 @@
 SIGMA_XY = 1.5
 SIGMA_Z = 1.0
 HALF = 4
-VMEM = 56 * 1024 * 1024
+RUN = 16
+PITCH = 24
+VMEM = 24 * 1024 * 1024
 
 
 def gaussian(sigma):
@@ -35,9 +37,10 @@
     return pltpu.CompilerParams(dimension_semantics=semantics, vmem_limit_bytes=VMEM)
 
 
-def register_kernel(first_ref, groups_ref, shifts_ref, x_ref, out_ref, aligned):
+def register_kernel(slots, first_ref, groups_ref, shifts_ref, x_ref, out_ref, aligned):
     frame = pl.program_id(0)
     planes, rows, width = x_ref.shape[1:]
+    cells = pl.ds(pl.multiple_of(pl.program_id(1) * 16, 16), 16)
     tile = rows // out_ref.shape[0]
     group = groups_ref[first_ref[0] + frame]
     shift_y, shift_x = shifts_ref[group, 0], shifts_ref[group, 1]
@@ -74,21 +77,22 @@
                 after = unit(plane, t * tile + tile - HALF)
                 ends.append(jnp.where(upper, after, before[plane]))
                 before[plane] = after
-            out_ref[t, 0, 0] = jnp.concatenate(ends, axis=0).astype(out_ref.dtype)
-            out_ref[t, 0, 1] = jnp.concatenate(middle, axis=0).astype(out_ref.dtype)
+            out_ref[slots[t], frame, 0, cells] = jnp.concatenate(ends, axis=0).astype(out_ref.dtype)
+            out_ref[slots[t], frame, 1, cells] = jnp.concatenate(middle, axis=0).astype(out_ref.dtype)
 
     pl.when(shift_y > 0.0)(lambda: finish(-1))
     pl.when(shift_y <= 0.0)(lambda: finish(1))
 
 
-def register(recording, group_ids, shifts, first, tiles):
+def register(recording, group_ids, shifts, first, slots):
+    tiles = len(slots)
     frames, planes, rows, width = recording.shape
     smem = pl.BlockSpec(memory_space=pltpu.SMEM)
     return pl.pallas_call(
-        register_kernel,
+        functools.partial(register_kernel, slots),
         grid=(frames, planes // 2),
         in_specs=[smem, smem, smem, pl.BlockSpec((1, 2, rows, width), lambda f, j: (f, j, 0, 0))],
-        out_specs=pl.BlockSpec((tiles, 1, 2, 16, width), lambda f, j: (0, f, 0, j, 0)),
+        out_specs=pl.BlockSpec(memory_space=pltpu.VMEM),
         out_shape=jax.ShapeDtypeStruct((tiles, frames, 2, planes * 8, width), recording.dtype),
         scratch_shapes=[pltpu.VMEM((2, rows + 16, width), jnp.float32)],
         cost_estimate=COST,
@@ -97,75 +101,69 @@
     )(first, group_ids, shifts, recording)
 
 
-def filter_kernel(part, taps_ref, x_ref, out_ref, low_ref, high_ref, *rest):
-    matrix, rows = rest[-2:]
-    frames, _, tile, width = x_ref.shape
-    planes = out_ref.shape[0]
+def filter_kernel(part, taps_ref, x_ref, *refs):
+    matrix, rows = refs[-2:]
+    out_ref, one, other = refs[-5:-2]
+    frames, _, cells, width = x_ref.shape
+    planes, tile = out_ref.shape[0], 16
     taps = taps_ref.shape[0]
     reach = (taps - 1) // 2
-    step = pl.program_id(0)
-
-    @pl.when(step == 0)
-    def _():
-        t = lax.broadcasted_iota(jnp.int32, (frames, frames), 0)
-        u = lax.broadcasted_iota(jnp.int32, (frames, frames), 1)
-        distance = u - t + reach
-        band = jnp.zeros((frames, frames), jnp.float32)
-        for k in range(taps):
-            band = jnp.where(distance == k, taps_ref[k], band)
-        matrix[...] = (band / jnp.sum(band, axis=1, keepdims=True)).astype(matrix.dtype)
-
-    rows[...] = x_ref[...].astype(jnp.float32).reshape(frames * tile, width)
-    weights = matrix[...]
-    for cell in range(tile):
-        values = rows[pl.ds(cell, frames, stride=tile), :]
-        baseline = jnp.dot(weights, values.astype(jnp.bfloat16), preferred_element_type=jnp.float32)
-        detrended = values - baseline
-        average = jnp.sum(detrended, axis=0, keepdims=True) * (1.0 / frames)
-        centred = detrended - average
-        power = jnp.sum(centred * centred, axis=0, keepdims=True) * (1.0 / frames)
-        out_ref[cell // 8, cell % 8] = (centred * lax.rsqrt(power + EPSILON)).astype(out_ref.dtype)
-    for p in range(planes):
-        plane = step * planes + p
-
-        @pl.when(plane < RADIUS)
-        def _():
-            low_ref[plane] = out_ref[p]
-
-        first = pl.num_programs(0) * planes - RADIUS
-
-        @pl.when(plane >= first)
-        def _():
-            high_ref[plane - first] = out_ref[p]
-
-        if part == 0:
-            rest[0][p] = out_ref[p, HALF - RADIUS : HALF]
-            rest[1][p] = out_ref[p, HALF : HALF + RADIUS]
-
-
-def filter_cells(registered, fir_taps, part):
+    t = lax.broadcasted_iota(jnp.int32, (frames, frames), 0)
+    u = lax.broadcasted_iota(jnp.int32, (frames, frames), 1)
+    distance = u - t + reach
+    band = jnp.zeros((frames, frames), jnp.float32)
+    for k in range(taps):
+        band = jnp.where(distance == k, taps_ref[k], band)
+    matrix[...] = (band / jnp.sum(band, axis=1, keepdims=True)).astype(matrix.dtype)
+
+    @pl.loop(0, cells // tile)
+    def _(step):
+        at = pl.multiple_of(step * tile, tile)
+        rows[:, :tile] = x_ref[:, part, pl.ds(at, tile)].astype(jnp.float32)
+        flat = rows.reshape(frames * PITCH, width)
+        weights = matrix[...]
+        for cell in range(tile):
+            values = flat[pl.ds(cell, frames, stride=PITCH), :]
+            baseline = jnp.dot(weights, values.astype(jnp.bfloat16), preferred_element_type=jnp.float32)
+            detrended = values - baseline
+            average = jnp.sum(detrended, axis=0, keepdims=True) * (1.0 / frames)
+            centred = detrended - average
+            power = jnp.sum(centred * centred, axis=0, keepdims=True) * (1.0 / frames)
+            plane, row = step * 2 + cell // 8, cell % 8
+            normed = (centred * lax.rsqrt(power + EPSILON)).astype(out_ref.dtype)
+            out_ref[plane, row] = normed
+            if part == 0 and HALF - RADIUS <= row < HALF:
+                one[plane, row - (HALF - RADIUS)] = normed
+            if part == 0 and HALF <= row < HALF + RADIUS:
+                other[plane, row - HALF] = normed
+
+    if part == 1:
+        ends = refs[0]
+        for k in range(RADIUS):
+            for slab, plane in ((one, planes - RADIUS + k), (other, k)):
+                slab[k, :8] = ends[plane]
+                slab[k, 8:] = out_ref[plane]
+
+
+def filter_cells(registered, fir_taps, part, *before):
     frames, _, cells, width = registered.shape
     planes = cells // 8
 
     def shape(*size):
         return jax.ShapeDtypeStruct((*size, frames, width), registered.dtype)
 
-    slab = pl.BlockSpec((RADIUS, 8, frames, width), lambda z: (0, 0, 0, 0))
-    rows = pl.BlockSpec((2, RADIUS, frames, width), lambda z: (z, 0, 0, 0))
+    halo = shape(planes, RADIUS) if part == 0 else shape(RADIUS, 16)
+    vmem = pl.BlockSpec(memory_space=pltpu.VMEM)
     return pl.pallas_call(
         functools.partial(filter_kernel, part),
-        grid=(planes // 2,),
-        in_specs=[
-            pl.BlockSpec(memory_space=pltpu.SMEM),
-            pl.BlockSpec((frames, 1, 16, width), lambda z: (0, part, z, 0)),
-        ],
-        out_specs=[pl.BlockSpec((2, 8, frames, width), lambda z: (z, 0, 0, 0)), slab, slab] + [rows, rows][: 2 - 2 * part],
-        out_shape=[shape(planes, 8), shape(RADIUS, 8), shape(RADIUS, 8)] + [shape(planes, RADIUS)] * (2 - 2 * part),
-        scratch_shapes=[pltpu.VMEM((frames, frames), jnp.bfloat16), pltpu.VMEM((frames * 16, width), jnp.float32)],
+        in_specs=[pl.BlockSpec(memory_space=pltpu.SMEM), vmem] + [vmem] * len(before),
+        out_specs=[vmem] * 3,
+        out_shape=[shape(planes, 8), halo, halo],
+        scratch_shapes=[pltpu.VMEM((frames, frames), jnp.bfloat16), pltpu.VMEM((frames, PITCH, width), jnp.float32)],
         cost_estimate=COST,
-        compiler_params=params("arbitrary"),
+        compiler_params=params(),
         name="filter",
-    )(fir_taps, registered)
+    )(fir_taps, registered, *before)
 
 
 def pair_sums(parts, taps):
@@ -178,7 +176,6 @@
 TAPS_Y = [float(v) for v in KERNEL_Y]
 TAPS_Z = [float(v) for v in KERNEL_Z]
 WINDOW = 2 * RADIUS + 1
-SCRATCH = 16
 
 
 def smooth_z(current, target):
@@ -209,7 +206,7 @@
         out_ref[z, pl.ds(y, 1), :] = total * (1.0 / (frames * (1.0 - CENTER)))
 
 
-def inner_kernel(ends, middle, low_ends, high_ends, low_middle, high_middle, out_ref, part_ref, *scratch):
+def inner_kernel(ends, middle, low, high, out_ref, part_ref, *scratch):
     current, ring, mixed, values, matrix = scratch
     planes, tile = out_ref.shape[0], out_ref.shape[1]
     frames = current.shape[1]
@@ -221,15 +218,17 @@
         inside = (y >= HALF) & (y < tile - HALF)
         row = jnp.where(inside, y - HALF, jnp.where(y < HALF, y + HALF, y - (tile - HALF)))
 
-        def fill(low, own, high):
+        beside = jnp.where(inside, 8, 0)
+
+        def fill(own):
             for k in range(RADIUS):
-                current[k] = low[k, row]
-                current[RADIUS + planes + k] = high[k, row]
+                current[k] = low[k, row + beside]
+                current[RADIUS + planes + k] = high[k, row + beside]
             for z in range(planes):
                 current[RADIUS + z] = own[z, row]
 
-        pl.when(inside)(lambda: fill(low_middle, middle, high_middle))
-        pl.when(jnp.logical_not(inside))(lambda: fill(low_ends, ends, high_ends))
+        pl.when(inside)(lambda: fill(middle))
+        pl.when(jnp.logical_not(inside))(lambda: fill(ends))
         smooth_z(current, ring.at[lax.rem(y + RADIUS, WINDOW)])
 
     def rows_of(y, z, start):
@@ -309,12 +308,12 @@
     side(low_corners, above, high_corners, RADIUS, 1)
 
 
-def inner(ends, middle, slabs_ends, slabs_middle, tile):
+def inner(ends, middle, slabs, tile):
     planes, _, frames, width = ends.shape
     vmem = pl.BlockSpec(memory_space=pltpu.VMEM)
     return pl.pallas_call(
         inner_kernel,
-        in_specs=[vmem] * 6,
+        in_specs=[vmem] * 4,
         out_specs=[vmem] * 2,
         out_shape=[
             jax.ShapeDtypeStruct((planes, tile, width), jnp.float32),
@@ -328,9 +327,9 @@
             pltpu.VMEM((width, width), jnp.bfloat16),
         ],
         cost_estimate=COST,
-        compiler_params=pltpu.CompilerParams(vmem_limit_bytes=SCRATCH * 2**21),
+        compiler_params=params(),
         name="inner",
-    )(ends, middle, *slabs_ends, *slabs_middle)
+    )(ends, middle, *slabs)
 
 
 def outer(ends, part, image, below, above, corners):
@@ -348,7 +347,7 @@
             pltpu.VMEM((width, width), jnp.bfloat16),
         ],
         cost_estimate=COST,
-        compiler_params=pltpu.CompilerParams(vmem_limit_bytes=SCRATCH * 2**21),
+        compiler_params=params(),
         name="outer",
     )(ends, part, image, below, above, *corners)
 
@@ -359,25 +358,26 @@
     tile = rows // tiles
     first = (lax.axis_index("frames") * recording.shape[0]).reshape(1)
 
+    slots = [t if t // RUN % 2 == 0 else t // RUN * RUN + RUN - 1 - t % RUN for t in range(tiles)]
+
     def shift(array, axis, by):
-        count = lax.axis_size(axis)
-        return lax.ppermute(array, axis, [(i, i + by) for i in range(count) if 0 <= i + by < count])
-
-    sent = register(recording, group_ids, shifts, first, tiles)
+        places = slots if axis == "frames" else list(range(lax.axis_size(axis)))
+        return lax.ppermute(array, axis, [(p, places[i + by]) for i, p in enumerate(places) if 0 <= i + by < len(places)])
+
+    sent = register(recording, group_ids, shifts, first, slots)
     arrived = lax.all_to_all(sent, "frames", 0, 0)
     arrived = arrived.reshape(-1, *arrived.shape[2:])
-    ends, low_ends, high_ends, up, down = filter_cells(arrived, fir_taps, 0)
+    ends, up, down = filter_cells(arrived, fir_taps, 0)
     below, above = shift(up, "frames", 1), shift(down, "frames", -1)
-    slabs_ends = [shift(high_ends, "gz", 1), shift(low_ends, "gz", -1)]
-    middle, low_middle, high_middle = filter_cells(arrived, fir_taps, 1)
-    slabs_middle = [shift(high_middle, "gz", 1), shift(low_middle, "gz", -1)]
-    image, part = inner(ends, middle, slabs_ends, slabs_middle, tile)
-    part, below, above = lax.optimization_barrier((part, below, above))
+    middle, to_next, to_last = filter_cells(arrived, fir_taps, 1, ends)
+    slabs = [shift(to_next, "gz", 1), shift(to_last, "gz", -1)]
+    image, part = inner(ends, middle, slabs, tile)
     corners = []
     for at, by in ((planes - RADIUS, 1), (0, -1)):
         both = jnp.concatenate([below[at : at + RADIUS], above[at : at + RADIUS]], axis=1)
         corners.append(shift(both, "gz", by))
-    return outer(ends, part, image, below, above, corners)
+    image = outer(ends, part, image, below, above, corners)
+    return lax.ppermute(image, "frames", [(p, t) for t, p in enumerate(slots)])
 
 
 def solution(mesh):

time: 212 us -> 188 us (0.89); the launches traced: 208 us -> 188 us
  Pallas kernels: 34.5 us -> 23.4 us
  starting transfers between devices: 37.1 us -> 28.1 us
    pallas_call x4, Pallas kernels: 31.1 us -> 20.6 us  [the longest x1 9.82 us: inner(): pl.pallas_call(inner_kernel, in_specs=[vmem] * 4, out_specs=[vmem] * 2, o...]
    ppermute x8 -> x7, starting transfers between devices: 37.1 us -> 28.1 us  [the longest x6 25.3 us: shift(): lax.ppermute(array, axis, [(p, places[i + by]) for i, p in enumerate(plac...]
    ppermute x8 -> x7, waiting for transfers between devices: 29.7 us -> 28.1 us  [the longest x6 22.6 us: shift(): lax.ppermute(array, axis, [(p, places[i + by]) for i, p in enumerate(plac...]
  transfers between devices with their start and end apart: 8 -> 7, of which waited for: 4 -> 3; matrix products, arithmetic and copies ran while one was open for 0% -> 0% of each run, Pallas kernels for 8% -> 7%
where the time goes in v1:
time: 188 us
  blocking collectives  103 us (55%)
  starting transfers between devices  28.1 us (15%)
  waiting for transfers between devices  28.1 us (15%)
  Pallas kernels  23.4 us (12%)
  local copies, waits for them, and re-layouts  4.32 us (2%)
    all_to_all x1, blocking collectives, body(): arrived = lax.all_to_all(sent, 'frames', 0, 0)  103 us
    ppermute x6, starting transfers between devices, shift(): lax.ppermute(array, axis, [(p, places[i + by]) for i, p in enumerate(plac...  25.3 us
    ppermute x6, waiting for transfers between devices, shift(): lax.ppermute(array, axis, [(p, places[i + by]) for i, p in enumerate(plac...  22.6 us
    pallas_call x1, Pallas kernels, inner(): pl.pallas_call(inner_kernel, in_specs=[vmem] * 4, out_specs=[vmem] * 2, o...  9.82 us
    pallas_call x2, Pallas kernels, filter_cells(): pl.pallas_call(functools.partial(filter_kernel, part), in_specs=[pl.Block...  6.84 us
    ppermute x1, waiting for transfers between devices, body(): return lax.ppermute(image, 'frames', [(p, t) for t, p in enumerate(slots)])  5.54 us
    unnamed x8, local copies, waits for them, and re-layouts  4.23 us
    pallas_call x1, Pallas kernels, register(): pl.pallas_call(functools.partial(register_kernel, slots), grid=(frames, p...  3.95 us
  transfers between devices with their start and end apart: 7, of which 3 were waited for; matrix products, arithmetic and copies ran while one was open for 0% of the time, Pallas kernels for 7%

profile of v1, /device:TPU:65, one launch (start us, length us, event | category | flops | bytes accessed | tf_op | source)
XLA Modules:
  0.0 187.5 jit_solution(15984819276109395033)
XLA Ops:
  0.0 0.8 copy.5.shifts_ref
  0.8 0.0 copy-start
  0.8 2.2 %copy-done = bf16[2,8,1024,128]{3,2,1,0:T(8,128)(2,1)S(1)} copy-done((bf16[2,8,1024,128]{3,2,1,0:T(8,128)(2,1)S(1)}, bf16[2,8,1024,128]{3,2,1,0:T(8,128)(2,1)}, u32[]{:S(2)}) %copy-start) | copy-done | bytes 4194328
  2.9 0.0 copy-start.2
  2.9 0.7 copy-done.2
  3.6 4.0 %register.1 = bf16[64,2,2,64,128]{4,3,2,1,0:T(8,128)(2,1)S(1)} custom-call(s32[1]{0:T(128)} %bitcast.first_ref, s32[128]{0:T(128)S(1)} %copy-done.2, f32[16,2]{1,0:T(8,128)S(1)} %copy.5.shifts_ref, bf16[2,8,1024,128]{3,2,1,0:T(8,128)(2,1)S(1)} %copy-done), custom_call_target="tpu_custom_call" | custom-call | flops 1 | bytes 1 | tf_op jit(solution)/shard_map/register/pallas_call | solution.py:91
  7.6 0.0 copy-start.1
  7.6 103.3 %all_to_all.5 = bf16[64,2,2,64,128]{4,3,2,1,0:T(8,128)(2,1)S(1)} all-to-all(bf16[64,2,2,64,128]{4,3,2,1,0:T(8,128)(2,1)S(1)} %register.1), channel_id=1, replica_groups=mesh['frames'=64,'gz'=4] {'frames'}, dimensions={0} | all-to-all | bytes 8388608 | tf_op jit(solution)/shard_map/all_to_all | solution.py:368
  110.8 0.0 copy-done.1
  110.8 3.3 %filter.2 = (bf16[8,8,128,128]{3,2,1,0:T(8,128)(2,1)S(1)}, bf16[8,3,128,128]{3,2,1,0:T(8,128)(2,1)S(1)}, bf16[8,3,128,128]{3,2,1,0:T(8,128)(2,1)S(1)}) custom-call(f32[31]{0:T(128)S(1)} %copy-done.1, bf16[128,2,64,128]{3,2,1,0:T(8,128)(2,1)S(1)} %bitcast.2), custom_call_target="tpu_custom_call" | custom-call | flops 1 | bytes 1 | tf_op jit(solution)/shard_map/filter/pallas_call | solution.py:157
  114.2 3.7 %collective-permute-start.2 = (bf16[8,3,128,128]{3,2,1,0:T(8,128)(2,1)S(1)}, bf16[8,3,128,128]{3,2,1,0:T(8,128)(2,1)S(1)}, u32[]{:S(2)}, u32[]{:S(2)}) collective-permute-start(bf16[8,3,128,128]{3,2,1,0:T(8,128)(2,1)S(1)} %get-tuple-element.19), channel_id=1, source_target_pairs={{0,4},{4,8},{8,12},{12,16},{16,20},{20,24},{24,28},{28,32},{32,36}... | collective-permute-start | bytes 2359304 | tf_op jit(solution)/shard_map/ppermute | solution.py:365
  117.9 2.5 %collective-permute-start.3 = (bf16[8,3,128,128]{3,2,1,0:T(8,128)(2,1)S(1)}, bf16[8,3,128,128]{3,2,1,0:T(8,128)(2,1)S(1)}, u32[]{:S(2)}, u32[]{:S(2)}) collective-permute-start(bf16[8,3,128,128]{3,2,1,0:T(8,128)(2,1)S(1)} %get-tuple-element.20), channel_id=1, source_target_pairs={{4,0},{8,4},{12,8},{16,12},{20,16},{24,20},{28,24},{32,28},{36,32}... | collective-permute-start | bytes 2359304 | tf_op jit(solution)/shard_map/ppermute | solution.py:365
  120.4 3.5 %filter.3 = (bf16[8,8,128,128]{3,2,1,0:T(8,128)(2,1)S(1)}, bf16[3,16,128,128]{3,2,1,0:T(8,128)(2,1)S(1)}, bf16[3,16,128,128]{3,2,1,0:T(8,128)(2,1)S(1)}) custom-call(f32[31]{0:T(128)S(1)} %copy-done.1, bf16[128,2,64,128]{3,2,1,0:T(8,128)(2,1)S(1)} %bitcast.3, bf16[8,8,128,128]{3,2,1,0:T(8,128)(2,1)S(1)} %get-tuple-element.13.refs_0_.ends), custom_call_target="tpu_custom_call" | custom-call | flops 1 | bytes 1 | tf_op jit(solution)/shard_map/filter/pallas_call | solution.py:157
  123.9 9.6 %collective-permute-start = (bf16[3,16,128,128]{3,2,1,0:T(8,128)(2,1)S(1)}, bf16[3,16,128,128]{3,2,1,0:T(8,128)(2,1)S(1)}, u32[]{:S(2)}, u32[]{:S(2)}) collective-permute-start(bf16[3,16,128,128]{3,2,1,0:T(8,128)(2,1)S(1)} %get-tuple-element.15), channel_id=1, source_target_pairs={{0,1},{1,2},{2,3},{4,5},{5,6},{6,7},{8,9},{9,10},{10,11},{12,13},{... | collective-permute-start | bytes 4718600 | tf_op jit(solution)/shard_map/ppermute | solution.py:365
  133.6 1.9 %collective-permute-start.1 = (bf16[3,16,128,128]{3,2,1,0:T(8,128)(2,1)S(1)}, bf16[3,16,128,128]{3,2,1,0:T(8,128)(2,1)S(1)}, u32[]{:S(2)}, u32[]{:S(2)}) collective-permute-start(bf16[3,16,128,128]{3,2,1,0:T(8,128)(2,1)S(1)} %get-tuple-element.16), channel_id=1, source_target_pairs={{1,0},{2,1},{3,2},{5,4},{6,5},{7,6},{9,8},{10,9},{11,10},{13,12},{... | collective-permute-start | bytes 4718600 | tf_op jit(solution)/shard_map/ppermute | solution.py:365
  135.5 0.0 collective-permute-done.2.refs_0_
  135.5 18.9 %collective-permute-done.3.refs_1_ = bf16[8,3,128,128]{3,2,1,0:T(8,128)(2,1)S(1)} collective-permute-done((bf16[8,3,128,128]{3,2,1,0:T(8,128)(2,1)S(1)}, bf16[8,3,128,128]{3,2,1,0:T(8,128)(2,1)S(1)}, u32[]{:S(2)}, u32[]{:S(2)}) %collective-permute-start.3) | collective-permute-done | bytes 786464 | tf_op jit(solution)/shard_map/ppermute | solution.py:365
  154.5 0.1 pad_maximum_fusion
  154.6 1.9 %collective-permute-start.4 = (bf16[3,6,128,128]{3,2,1,0:T(8,128)(2,1)S(1)}, bf16[3,6,128,128]{3,2,1,0:T(8,128)(2,1)S(1)}, u32[]{:S(2)}, u32[]{:S(2)}) collective-permute-start(bf16[3,6,128,128]{3,2,1,0:T(8,128)(2,1)S(1)} %pad_maximum_fusion), channel_id=1, source_target_pairs={{0,1},{1,2},{2,3},{4,5},{5,6},{6,7},{8,9},{9,10},{10,11},{12,13},{... | collective-permute-start | bytes 1769480 | tf_op jit(solution)/shard_map/ppermute | solution.py:365
  156.5 0.1 pad_maximum_fusion.1
  156.6 5.7 %collective-permute-start.5 = (bf16[3,6,128,128]{3,2,1,0:T(8,128)(2,1)S(1)}, bf16[3,6,128,128]{3,2,1,0:T(8,128)(2,1)S(1)}, u32[]{:S(2)}, u32[]{:S(2)}) collective-permute-start(bf16[3,6,128,128]{3,2,1,0:T(8,128)(2,1)S(1)} %pad_maximum_fusion.1), channel_id=1, source_target_pairs={{1,0},{2,1},{3,2},{5,4},{6,5},{7,6},{9,8},{10,9},{11,10},{13,12},{... | collective-permute-start | bytes 1769480 | tf_op jit(solution)/shard_map/ppermute | solution.py:365
  162.3 0.0 collective-permute-done.low
  162.3 3.6 %collective-permute-done.1.high = bf16[3,16,128,128]{3,2,1,0:T(8,128)(2,1)S(1)} collective-permute-done((bf16[3,16,128,128]{3,2,1,0:T(8,128)(2,1)S(1)}, bf16[3,16,128,128]{3,2,1,0:T(8,128)(2,1)S(1)}, u32[]{:S(2)}, u32[]{:S(2)}) %collective-permute-start.1) | collective-permute-done | bytes 1572896 | tf_op jit(solution)/shard_map/ppermute | solution.py:365
  165.9 9.8 %inner.1 = (f32[8,16,128]{2,1,0:T(8,128)S(1)}, f32[6,8,128,128]{3,2,1,0:T(8,128)S(1)}) custom-call(bf16[8,8,128,128]{3,2,1,0:T(8,128)(2,1)S(1)} %get-tuple-element.13.refs_0_.ends, bf16[8,8,128,128]{3,2,1,0:T(8,128)(2,1)S(1)} %get-tuple-element.14.middle, bf16[3,16,128,128]{3,2,1,0:T(8,128)(2,1)S(1)} %collective-permute-done.low, ...), custom_call_target="tpu_custom_call" | custom-call | flops 1 | bytes 1 | tf_op jit(solution)/shard_map/inner/pallas_call | solution.py:314
  175.7 0.0 collective-permute-done.4.refs_2_
  175.7 0.0 collective-permute-done.5.refs_3_
  175.8 2.8 %outer.1 = f32[8,16,128]{2,1,0:T(8,128)S(1)} custom-call(bf16[8,8,128,128]{3,2,1,0:T(8,128)(2,1)S(1)} %get-tuple-element.13.refs_0_.ends, f32[6,8,128,128]{3,2,1,0:T(8,128)S(1)} %get-tuple-element.17.part, f32[8,16,128]{2,1,0:T(8,128)S(1)} %get-tuple-element.18.image, bf16[8,3,128,128]{3,2,1,0:T(8,128)(2,1)S(1)} %collective-permute-done.2.refs_0_, ...), custom_call_target="tpu_custom_call" | custom-call | flops 1 | bytes 1 | tf_op jit(solution)/shard_map/outer/pallas_call | solution.py:338
  178.5 2.8 %collective-permute-start.6 = (f32[8,16,128]{2,1,0:T(8,128)S(1)}, f32[8,16,128]{2,1,0:T(8,128)S(1)}, u32[]{:S(2)}, u32[]{:S(2)}) collective-permute-start(f32[8,16,128]{2,1,0:T(8,128)S(1)} %outer.1), channel_id=1, source_target_pairs={{0,0},{4,4},{8,8},{12,12},{16,16},{20,20},{24,24},{28,28},{32,32},... | collective-permute-start | bytes 196616 | tf_op jit(solution)/shard_map/ppermute | solution.py:380
  181.3 5.5 %collective-permute-done.6 = f32[8,16,128]{2,1,0:T(8,128)S(1)} collective-permute-done((f32[8,16,128]{2,1,0:T(8,128)S(1)}, f32[8,16,128]{2,1,0:T(8,128)S(1)}, u32[]{:S(2)}, u32[]{:S(2)}) %collective-permute-start.6) | collective-permute-done | bytes 65568 | tf_op jit(solution)/shard_map/ppermute | solution.py:380
  186.9 0.6 copy.7
  (2 shorter events, 0.1 us)
Async XLA Ops:
  0.8 2.2 %copy-start = (bf16[2,8,1024,128]{3,2,1,0:T(8,128)(2,1)S(1)}, bf16[2,8,1024,128]{3,2,1,0:T(8,128)(2,1)}, u32[]{:S(2)}) copy-start(bf16[2,8,1024,128]{3,2,1,0:T(8,128)(2,1)} %x_ref.1) | copy-start | bytes 12582916
  2.9 0.7 copy-start.2
  7.6 103.3 %copy-start.1 = (f32[31]{0:T(128)S(1)}, f32[31]{0:T(128)}, u32[]{:S(2)}) copy-start(f32[31]{0:T(128)} %taps_ref.3) | copy-start | bytes 376
  114.2 21.3 %collective-permute-start.2 = (bf16[8,3,128,128]{3,2,1,0:T(8,128)(2,1)S(1)}, bf16[8,3,128,128]{3,2,1,0:T(8,128)(2,1)S(1)}, u32[]{:S(2)}, u32[]{:S(2)}) collective-permute-start(bf16[8,3,128,128]{3,2,1,0:T(8,128)(2,1)S(1)} %get-tuple-element.19), channel_id=1, source_target_pairs={{0,4},{4,8},{8,12},{12,16},{16,20},{20,24},{24,28},{28,32},{32,36}... | collective-permute-start | bytes 2359304 | tf_op jit(solution)/shard_map/ppermute | solution.py:365
  117.9 36.6 %collective-permute-start.3 = (bf16[8,3,128,128]{3,2,1,0:T(8,128)(2,1)S(1)}, bf16[8,3,128,128]{3,2,1,0:T(8,128)(2,1)S(1)}, u32[]{:S(2)}, u32[]{:S(2)}) collective-permute-start(bf16[8,3,128,128]{3,2,1,0:T(8,128)(2,1)S(1)} %get-tuple-element.20), channel_id=1, source_target_pairs={{4,0},{8,4},{12,8},{16,12},{20,16},{24,20},{28,24},{32,28},{36,32}... | collective-permute-start | bytes 2359304 | tf_op jit(solution)/shard_map/ppermute | solution.py:365
  123.9 38.3 %collective-permute-start = (bf16[3,16,128,128]{3,2,1,0:T(8,128)(2,1)S(1)}, bf16[3,16,128,128]{3,2,1,0:T(8,128)(2,1)S(1)}, u32[]{:S(2)}, u32[]{:S(2)}) collective-permute-start(bf16[3,16,128,128]{3,2,1,0:T(8,128)(2,1)S(1)} %get-tuple-element.15), channel_id=1, source_target_pairs={{0,1},{1,2},{2,3},{4,5},{5,6},{6,7},{8,9},{9,10},{10,11},{12,13},{... | collective-permute-start | bytes 4718600 | tf_op jit(solution)/shard_map/ppermute | solution.py:365
  133.6 32.3 %collective-permute-start.1 = (bf16[3,16,128,128]{3,2,1,0:T(8,128)(2,1)S(1)}, bf16[3,16,128,128]{3,2,1,0:T(8,128)(2,1)S(1)}, u32[]{:S(2)}, u32[]{:S(2)}) collective-permute-start(bf16[3,16,128,128]{3,2,1,0:T(8,128)(2,1)S(1)} %get-tuple-element.16), channel_id=1, source_target_pairs={{1,0},{2,1},{3,2},{5,4},{6,5},{7,6},{9,8},{10,9},{11,10},{13,12},{... | collective-permute-start | bytes 4718600 | tf_op jit(solution)/shard_map/ppermute | solution.py:365
  154.6 21.1 %collective-permute-start.4 = (bf16[3,6,128,128]{3,2,1,0:T(8,128)(2,1)S(1)}, bf16[3,6,128,128]{3,2,1,0:T(8,128)(2,1)S(1)}, u32[]{:S(2)}, u32[]{:S(2)}) collective-permute-start(bf16[3,6,128,128]{3,2,1,0:T(8,128)(2,1)S(1)} %pad_maximum_fusion), channel_id=1, source_target_pairs={{0,1},{1,2},{2,3},{4,5},{5,6},{6,7},{8,9},{9,10},{10,11},{12,13},{... | collective-permute-start | bytes 1769480 | tf_op jit(solution)/shard_map/ppermute | solution.py:365
  156.6 19.2 %collective-permute-start.5 = (bf16[3,6,128,128]{3,2,1,0:T(8,128)(2,1)S(1)}, bf16[3,6,128,128]{3,2,1,0:T(8,128)(2,1)S(1)}, u32[]{:S(2)}, u32[]{:S(2)}) collective-permute-start(bf16[3,6,128,128]{3,2,1,0:T(8,128)(2,1)S(1)} %pad_maximum_fusion.1), channel_id=1, source_target_pairs={{1,0},{2,1},{3,2},{5,4},{6,5},{7,6},{9,8},{10,9},{11,10},{13,12},{... | collective-permute-start | bytes 1769480 | tf_op jit(solution)/shard_map/ppermute | solution.py:365
  178.5 8.3 %collective-permute-start.6 = (f32[8,16,128]{2,1,0:T(8,128)S(1)}, f32[8,16,128]{2,1,0:T(8,128)S(1)}, u32[]{:S(2)}, u32[]{:S(2)}) collective-permute-start(f32[8,16,128]{2,1,0:T(8,128)S(1)} %outer.1), channel_id=1, source_target_pairs={{0,0},{4,4},{8,8},{12,12},{16,16},{20,20},{24,24},{28,28},{32,32},... | collective-permute-start | bytes 196616 | tf_op jit(solution)/shard_map/ppermute | solution.py:380

commit v2 on v1

--- a/solution.py
+++ b/solution.py
@@ -167,128 +167,134 @@
 
 
 def pair_sums(parts, taps):
-    total = taps[RADIUS] * parts[RADIUS]
+    total = parts[RADIUS]
     for k in range(RADIUS):
         total = total + taps[k] * (parts[k] + parts[2 * RADIUS - k])
     return total
 
 
-TAPS_Y = [float(v) for v in KERNEL_Y]
-TAPS_Z = [float(v) for v in KERNEL_Z]
+TAPS_Y = [float(v / KERNEL_Y[RADIUS]) for v in KERNEL_Y]
+TAPS_Z = [float(v / KERNEL_Z[RADIUS]) for v in KERNEL_Z]
+SCALE = float(KERNEL_Z[RADIUS]) * float(KERNEL_Y[RADIUS])
 WINDOW = 2 * RADIUS + 1
 
 
-def smooth_z(current, target):
-    planes = target.shape[0]
-    for start in range(0, current.shape[1], 16):
-        parts = [current[z, start : start + 16].astype(jnp.float32) for z in range(planes + 2 * RADIUS)]
+def smooth_z(rows, target):
+    planes, frames = target.shape[0], target.shape[1]
+    for start in range(0, frames, 16):
+        parts = [ref[z, row, start : start + 16].astype(jnp.float32) for ref, z, row in rows]
         for z in range(planes):
             target[z, start : start + 16] = pair_sums(parts[z : z + WINDOW], TAPS_Z)
 
 
+def stack(low, own, high, planes, low_row, own_row, high_row):
+    rows = [(low, k, low_row) for k in range(RADIUS)]
+    rows += [(own, z, own_row) for z in range(planes)]
+    return rows + [(high, k, high_row) for k in range(RADIUS)]
+
+
 def band_of(matrix):
-    width = matrix.shape[0]
+    width = matrix.shape[1]
     distance = lax.broadcasted_iota(jnp.int32, (width, width), 1) - lax.broadcasted_iota(
         jnp.int32, (width, width), 0
     )
     band = jnp.zeros((width, width), jnp.float32)
     for k in range(WINDOW):
         band = jnp.where(distance == k - RADIUS, float(KERNEL_X[k]), band)
-    matrix[...] = band.astype(matrix.dtype)
+    matrix[:width] = band.astype(matrix.dtype)
+    matrix[width:] = jnp.where(distance == 0, -float(KERNEL_X[RADIUS]), 0.0).astype(matrix.dtype)
 
 
 def row_of_image(mixed, values_of, matrix, out_ref, y):
     for z in range(mixed.shape[0]):
-        smoothed = jnp.dot(mixed[z], matrix[...], preferred_element_type=jnp.float32)
-        values = values_of(z).astype(jnp.float32)
-        frames = values.shape[0]
-        total = jnp.sum(values * (smoothed - CENTER * values), axis=0, keepdims=True)
-        out_ref[z, pl.ds(y, 1), :] = total * (1.0 / (frames * (1.0 - CENTER)))
+        values = values_of(z)
+        both = jnp.concatenate([mixed[z], values], axis=1)
+        neighbor = jnp.dot(both, matrix[...], preferred_element_type=jnp.float32)
+        total = jnp.sum(values.astype(jnp.float32) * neighbor, axis=0, keepdims=True)
+        out_ref[z, pl.ds(y, 1), :] = total * (SCALE / (values.shape[0] * (1.0 - CENTER)))
 
 
 def inner_kernel(ends, middle, low, high, out_ref, part_ref, *scratch):
-    current, ring, mixed, values, matrix = scratch
+    ring, mixed, matrix = scratch
     planes, tile = out_ref.shape[0], out_ref.shape[1]
-    frames = current.shape[1]
+    frames = ring.shape[2]
     band_of(matrix)
     for row in range(RADIUS):
         ring[row] = jnp.zeros(ring.shape[1:], ring.dtype)
 
-    def take(y):
-        inside = (y >= HALF) & (y < tile - HALF)
-        row = jnp.where(inside, y - HALF, jnp.where(y < HALF, y + HALF, y - (tile - HALF)))
-
-        beside = jnp.where(inside, 8, 0)
-
-        def fill(own):
-            for k in range(RADIUS):
-                current[k] = low[k, row + beside]
-                current[RADIUS + planes + k] = high[k, row + beside]
-            for z in range(planes):
-                current[RADIUS + z] = own[z, row]
-
-        pl.when(inside)(lambda: fill(middle))
-        pl.when(jnp.logical_not(inside))(lambda: fill(ends))
-        smooth_z(current, ring.at[lax.rem(y + RADIUS, WINDOW)])
-
-    def rows_of(y, z, start):
-        return pair_sums([ring[lax.rem(y + k, WINDOW), z, start : start + 32] for k in range(WINDOW)], TAPS_Y)
+    def first_ends(y):
+        return ends, y + HALF, y + HALF
+
+    def inside(y):
+        return middle, y - HALF, y + HALF
+
+    def last_ends(y):
+        return ends, y - (tile - HALF), y - (tile - HALF)
+
+    def slot(y):
+        return lax.rem(y + RADIUS, ring.shape[0])
+
+    def take(y, where):
+        own, row, beside = where(y)
+        smooth_z(stack(low, own, high, planes, beside, row, beside), ring.at[slot(y)])
 
     def give_part(y, at):
         for z in range(planes):
             for start in range(0, frames, 32):
-                part_ref[at, z, start : start + 32] = rows_of(y, z, start)
-
-    def give(y):
-        inside = (y >= HALF) & (y < tile - HALF)
-        row = jnp.where(inside, y - HALF, jnp.where(y < HALF, y + HALF, y - (tile - HALF)))
-
-        def fill(own):
-            for z in range(planes):
-                values[z] = own[z, row]
-
-        pl.when(inside)(lambda: fill(middle))
-        pl.when(jnp.logical_not(inside))(lambda: fill(ends))
+                parts = [ring[slot(y + k - RADIUS), z, start : start + 32] for k in range(WINDOW)]
+                part_ref[at, z, start : start + 32] = pair_sums(parts, TAPS_Y)
+
+    def give_two(y, *where):
         for z in range(planes):
             for start in range(0, frames, 32):
-                mixed[z, start : start + 32] = rows_of(y, z, start).astype(mixed.dtype)
-        row_of_image(mixed, lambda z: values[z], matrix, out_ref, y)
-
-    pl.loop(0, RADIUS)(take)
+                parts = [ring[slot(y + k - RADIUS), z, start : start + 32] for k in range(WINDOW + 1)]
+                for n in range(2):
+                    total = pair_sums(parts[n : n + WINDOW], TAPS_Y)
+                    mixed[n, z, start : start + 32] = total.astype(mixed.dtype)
+        for n in range(2):
+            own, row, _ = where[n](y + n)
+            row_of_image(mixed.at[n], lambda z, own=own, row=row: own[z, row], matrix, out_ref, y + n)
+
+    def run(begin, end, taken, *given):
+        @pl.loop(0, (end - begin) // 2)
+        def _(i):
+            y = begin + 2 * i
+            take(y, taken)
+            take(y + 1, taken)
+            if given:
+                give_two(y - RADIUS, *given)
+
+    turn = tile - HALF
+    pl.loop(0, RADIUS)(lambda y: take(y, first_ends))
 
     @pl.loop(RADIUS, 2 * RADIUS)
     def _(y):
-        take(y)
+        pl.when(y < HALF)(lambda: take(y, first_ends))
+        pl.when(y >= HALF)(lambda: take(y, inside))
         give_part(y - RADIUS, y - RADIUS)
 
-    @pl.loop(2 * RADIUS, tile)
-    def _(y):
-        take(y)
-        give(y - RADIUS)
+    run(2 * RADIUS, 2 * RADIUS + 2, inside, first_ends, inside)
+    run(2 * RADIUS + 2, turn, inside, inside, inside)
+    run(turn, turn + 2, last_ends, inside, inside)
+    run(turn + 2, tile, last_ends, inside, last_ends)
 
     @pl.loop(tile, tile + RADIUS)
     def _(y):
-        slot = lax.rem(y + RADIUS, WINDOW)
-        ring[slot] = jnp.zeros(ring.shape[1:], ring.dtype)
+        ring[slot(y)] = jnp.zeros(ring.shape[1:], ring.dtype)
         give_part(y - RADIUS, y - tile + RADIUS)
 
 
 def outer_kernel(ends, part, image, *refs):
-    sides, (out_ref, current, halo, mixed, matrix) = refs[:-5], refs[-5:]
+    sides, (out_ref, halo, mixed, matrix) = refs[:-4], refs[-4:]
     planes, tile = out_ref.shape[0], out_ref.shape[1]
-    frames = current.shape[1]
+    frames = halo.shape[2]
     band_of(matrix)
     out_ref[...] = image[...]
 
     def side(low, own, high, first, upper):
         @pl.loop(0, RADIUS)
         def _(k):
-            for j in range(RADIUS):
-                current[j] = low[j, first + k]
-                current[RADIUS + planes + j] = high[j, first + k]
-            for z in range(planes):
-                current[RADIUS + z] = own[z, k]
-            smooth_z(current, halo.at[k])
+            smooth_z(stack(low, own, high, planes, first + k, k, first + k), halo.at[k])
 
         for n in range(RADIUS):
             y = tile - RADIUS + n if upper else n
@@ -320,11 +326,9 @@
             jax.ShapeDtypeStruct((2 * RADIUS, planes, frames, width), jnp.float32),
         ],
         scratch_shapes=[
-            pltpu.VMEM((planes + 2 * RADIUS, frames, width), jnp.bfloat16),
-            pltpu.VMEM((WINDOW, planes, frames, width), jnp.float32),
-            pltpu.VMEM((planes, frames, width), jnp.bfloat16),
-            pltpu.VMEM((planes, frames, width), jnp.bfloat16),
-            pltpu.VMEM((width, width), jnp.bfloat16),
+            pltpu.VMEM((WINDOW + 1, planes, frames, width), jnp.float32),
+            pltpu.VMEM((2, planes, frames, width), jnp.bfloat16),
+            pltpu.VMEM((2 * width, width), jnp.bfloat16),
         ],
         cost_estimate=COST,
         compiler_params=params(),
@@ -341,10 +345,9 @@
         out_specs=vmem,
         out_shape=jax.ShapeDtypeStruct(image.shape, jnp.float32),
         scratch_shapes=[
-            pltpu.VMEM((planes + 2 * RADIUS, frames, width), jnp.bfloat16),
             pltpu.VMEM((RADIUS, planes, frames, width), jnp.float32),
             pltpu.VMEM((planes, frames, width), jnp.bfloat16),
-            pltpu.VMEM((width, width), jnp.bfloat16),
+            pltpu.VMEM((2 * width, width), jnp.bfloat16),
         ],
         cost_estimate=COST,
         compiler_params=params(),

time: 188 us -> 186 us (0.989)
  transfers between devices with their start and end apart: 7 -> 7, of which waited for: 3 -> 3; matrix products, arithmetic and copies ran while one was open for 0% -> 0% of each run, Pallas kernels for 7% -> 6%
where the time goes in v2:
time: 186 us
  blocking collectives  103 us (55%)
  starting transfers between devices  28.1 us (15%)
  waiting for transfers between devices  28.1 us (15%)
  Pallas kernels  21.7 us (12%)
  local copies, waits for them, and re-layouts  4.32 us (2%)
    all_to_all x1, blocking collectives, body(): arrived = lax.all_to_all(sent, 'frames', 0, 0)  103 us
    ppermute x6, starting transfers between devices, shift(): lax.ppermute(array, axis, [(p, places[i + by]) for i, p in enumerate(plac...  25.3 us
    ppermute x6, waiting for transfers between devices, shift(): lax.ppermute(array, axis, [(p, places[i + by]) for i, p in enumerate(plac...  22.6 us
    pallas_call x1, Pallas kernels, inner(): pl.pallas_call(inner_kernel, in_specs=[vmem] * 4, out_specs=[vmem] * 2, o...  8.27 us
    pallas_call x2, Pallas kernels, filter_cells(): pl.pallas_call(functools.partial(filter_kernel, part), in_specs=[pl.Block...  6.84 us
    ppermute x1, waiting for transfers between devices, body(): return lax.ppermute(image, 'frames', [(p, t) for t, p in enumerate(slots)])  5.54 us
    unnamed x8, local copies, waits for them, and re-layouts  4.23 us
    pallas_call x1, Pallas kernels, register(): pl.pallas_call(functools.partial(register_kernel, slots), grid=(frames, p...  3.93 us
  transfers between devices with their start and end apart: 7, of which 3 were waited for; matrix products, arithmetic and copies ran while one was open for 0% of the time, Pallas kernels for 6%

profile of v2, /device:TPU:65, one launch (start us, length us, event | category | flops | bytes accessed | tf_op | source)
XLA Modules:
  0.0 185.8 jit_solution(5986913904298773811)
XLA Ops:
  0.0 0.8 copy.5.shifts_ref
  0.8 0.0 copy-start
  0.8 2.2 %copy-done = bf16[2,8,1024,128]{3,2,1,0:T(8,128)(2,1)S(1)} copy-done((bf16[2,8,1024,128]{3,2,1,0:T(8,128)(2,1)S(1)}, bf16[2,8,1024,128]{3,2,1,0:T(8,128)(2,1)}, u32[]{:S(2)}) %copy-start) | copy-done | bytes 4194328
  2.9 0.0 copy-start.2
  2.9 0.7 copy-done.2
  3.6 3.9 %register.1 = bf16[64,2,2,64,128]{4,3,2,1,0:T(8,128)(2,1)S(1)} custom-call(s32[1]{0:T(128)} %bitcast.first_ref, s32[128]{0:T(128)S(1)} %copy-done.2, f32[16,2]{1,0:T(8,128)S(1)} %copy.5.shifts_ref, bf16[2,8,1024,128]{3,2,1,0:T(8,128)(2,1)S(1)} %copy-done), custom_call_target="tpu_custom_call" | custom-call | flops 1 | bytes 1 | tf_op jit(solution)/shard_map/register/pallas_call | solution.py:91
  7.5 0.0 copy-start.1
  7.6 103.3 %all_to_all.5 = bf16[64,2,2,64,128]{4,3,2,1,0:T(8,128)(2,1)S(1)} all-to-all(bf16[64,2,2,64,128]{4,3,2,1,0:T(8,128)(2,1)S(1)} %register.1), channel_id=1, replica_groups=mesh['frames'=64,'gz'=4] {'frames'}, dimensions={0} | all-to-all | bytes 8388608 | tf_op jit(solution)/shard_map/all_to_all | solution.py:371
  110.8 0.0 copy-done.1
  110.8 3.3 %filter.2 = (bf16[8,8,128,128]{3,2,1,0:T(8,128)(2,1)S(1)}, bf16[8,3,128,128]{3,2,1,0:T(8,128)(2,1)S(1)}, bf16[8,3,128,128]{3,2,1,0:T(8,128)(2,1)S(1)}) custom-call(f32[31]{0:T(128)S(1)} %copy-done.1, bf16[128,2,64,128]{3,2,1,0:T(8,128)(2,1)S(1)} %bitcast.2), custom_call_target="tpu_custom_call" | custom-call | flops 1 | bytes 1 | tf_op jit(solution)/shard_map/filter/pallas_call | solution.py:157
  114.2 3.7 %collective-permute-start.2 = (bf16[8,3,128,128]{3,2,1,0:T(8,128)(2,1)S(1)}, bf16[8,3,128,128]{3,2,1,0:T(8,128)(2,1)S(1)}, u32[]{:S(2)}, u32[]{:S(2)}) collective-permute-start(bf16[8,3,128,128]{3,2,1,0:T(8,128)(2,1)S(1)} %get-tuple-element.19), channel_id=1, source_target_pairs={{0,4},{4,8},{8,12},{12,16},{16,20},{20,24},{24,28},{28,32},{32,36}... | collective-permute-start | bytes 2359304 | tf_op jit(solution)/shard_map/ppermute | solution.py:368
  117.9 2.5 %collective-permute-start.3 = (bf16[8,3,128,128]{3,2,1,0:T(8,128)(2,1)S(1)}, bf16[8,3,128,128]{3,2,1,0:T(8,128)(2,1)S(1)}, u32[]{:S(2)}, u32[]{:S(2)}) collective-permute-start(bf16[8,3,128,128]{3,2,1,0:T(8,128)(2,1)S(1)} %get-tuple-element.20), channel_id=1, source_target_pairs={{4,0},{8,4},{12,8},{16,12},{20,16},{24,20},{28,24},{32,28},{36,32}... | collective-permute-start | bytes 2359304 | tf_op jit(solution)/shard_map/ppermute | solution.py:368
  120.4 3.5 %filter.3 = (bf16[8,8,128,128]{3,2,1,0:T(8,128)(2,1)S(1)}, bf16[3,16,128,128]{3,2,1,0:T(8,128)(2,1)S(1)}, bf16[3,16,128,128]{3,2,1,0:T(8,128)(2,1)S(1)}) custom-call(f32[31]{0:T(128)S(1)} %copy-done.1, bf16[128,2,64,128]{3,2,1,0:T(8,128)(2,1)S(1)} %bitcast.3, bf16[8,8,128,128]{3,2,1,0:T(8,128)(2,1)S(1)} %get-tuple-element.13.refs_0_.ends), custom_call_target="tpu_custom_call" | custom-call | flops 1 | bytes 1 | tf_op jit(solution)/shard_map/filter/pallas_call | solution.py:157
  123.9 9.6 %collective-permute-start = (bf16[3,16,128,128]{3,2,1,0:T(8,128)(2,1)S(1)}, bf16[3,16,128,128]{3,2,1,0:T(8,128)(2,1)S(1)}, u32[]{:S(2)}, u32[]{:S(2)}) collective-permute-start(bf16[3,16,128,128]{3,2,1,0:T(8,128)(2,1)S(1)} %get-tuple-element.15), channel_id=1, source_target_pairs={{0,1},{1,2},{2,3},{4,5},{5,6},{6,7},{8,9},{9,10},{10,11},{12,13},{... | collective-permute-start | bytes 4718600 | tf_op jit(solution)/shard_map/ppermute | solution.py:368
  133.5 1.9 %collective-permute-start.1 = (bf16[3,16,128,128]{3,2,1,0:T(8,128)(2,1)S(1)}, bf16[3,16,128,128]{3,2,1,0:T(8,128)(2,1)S(1)}, u32[]{:S(2)}, u32[]{:S(2)}) collective-permute-start(bf16[3,16,128,128]{3,2,1,0:T(8,128)(2,1)S(1)} %get-tuple-element.16), channel_id=1, source_target_pairs={{1,0},{2,1},{3,2},{5,4},{6,5},{7,6},{9,8},{10,9},{11,10},{13,12},{... | collective-permute-start | bytes 4718600 | tf_op jit(solution)/shard_map/ppermute | solution.py:368
  135.5 0.0 collective-permute-done.2.refs_0_
  135.5 18.9 %collective-permute-done.3.refs_1_ = bf16[8,3,128,128]{3,2,1,0:T(8,128)(2,1)S(1)} collective-permute-done((bf16[8,3,128,128]{3,2,1,0:T(8,128)(2,1)S(1)}, bf16[8,3,128,128]{3,2,1,0:T(8,128)(2,1)S(1)}, u32[]{:S(2)}, u32[]{:S(2)}) %collective-permute-start.3) | collective-permute-done | bytes 786464 | tf_op jit(solution)/shard_map/ppermute | solution.py:368
  154.5 0.1 pad_maximum_fusion
  154.6 1.9 %collective-permute-start.4 = (bf16[3,6,128,128]{3,2,1,0:T(8,128)(2,1)S(1)}, bf16[3,6,128,128]{3,2,1,0:T(8,128)(2,1)S(1)}, u32[]{:S(2)}, u32[]{:S(2)}) collective-permute-start(bf16[3,6,128,128]{3,2,1,0:T(8,128)(2,1)S(1)} %pad_maximum_fusion), channel_id=1, source_target_pairs={{0,1},{1,2},{2,3},{4,5},{5,6},{6,7},{8,9},{9,10},{10,11},{12,13},{... | collective-permute-start | bytes 1769480 | tf_op jit(solution)/shard_map/ppermute | solution.py:368
  156.5 0.1 pad_maximum_fusion.1
  156.6 5.7 %collective-permute-start.5 = (bf16[3,6,128,128]{3,2,1,0:T(8,128)(2,1)S(1)}, bf16[3,6,128,128]{3,2,1,0:T(8,128)(2,1)S(1)}, u32[]{:S(2)}, u32[]{:S(2)}) collective-permute-start(bf16[3,6,128,128]{3,2,1,0:T(8,128)(2,1)S(1)} %pad_maximum_fusion.1), channel_id=1, source_target_pairs={{1,0},{2,1},{3,2},{5,4},{6,5},{7,6},{9,8},{10,9},{11,10},{13,12},{... | collective-permute-start | bytes 1769480 | tf_op jit(solution)/shard_map/ppermute | solution.py:368
  162.2 0.0 collective-permute-done.low
  162.3 3.6 %collective-permute-done.1.high = bf16[3,16,128,128]{3,2,1,0:T(8,128)(2,1)S(1)} collective-permute-done((bf16[3,16,128,128]{3,2,1,0:T(8,128)(2,1)S(1)}, bf16[3,16,128,128]{3,2,1,0:T(8,128)(2,1)S(1)}, u32[]{:S(2)}, u32[]{:S(2)}) %collective-permute-start.1) | collective-permute-done | bytes 1572896 | tf_op jit(solution)/shard_map/ppermute | solution.py:368
  165.9 8.3 %inner.1 = (f32[8,16,128]{2,1,0:T(8,128)S(1)}, f32[6,8,128,128]{3,2,1,0:T(8,128)S(1)}) custom-call(bf16[8,8,128,128]{3,2,1,0:T(8,128)(2,1)S(1)} %get-tuple-element.13.refs_0_.ends, bf16[8,8,128,128]{3,2,1,0:T(8,128)(2,1)S(1)} %get-tuple-element.14.middle, bf16[3,16,128,128]{3,2,1,0:T(8,128)(2,1)S(1)} %collective-permute-done.low, ...), custom_call_target="tpu_custom_call" | custom-call | flops 1 | bytes 1 | tf_op jit(solution)/shard_map/inner/pallas_call | solution.py:320
  174.2 0.0 collective-permute-done.4.refs_2_
  174.2 0.0 collective-permute-done.5.refs_3_
  174.2 2.7 %outer.1 = f32[8,16,128]{2,1,0:T(8,128)S(1)} custom-call(bf16[8,8,128,128]{3,2,1,0:T(8,128)(2,1)S(1)} %get-tuple-element.13.refs_0_.ends, f32[6,8,128,128]{3,2,1,0:T(8,128)S(1)} %get-tuple-element.17.part, f32[8,16,128]{2,1,0:T(8,128)S(1)} %get-tuple-element.18.image, bf16[8,3,128,128]{3,2,1,0:T(8,128)(2,1)S(1)} %collective-permute-done.2.refs_0_, ...), custom_call_target="tpu_custom_call" | custom-call | flops 1 | bytes 1 | tf_op jit(solution)/shard_map/outer/pallas_call | solution.py:342
  176.9 2.8 %collective-permute-start.6 = (f32[8,16,128]{2,1,0:T(8,128)S(1)}, f32[8,16,128]{2,1,0:T(8,128)S(1)}, u32[]{:S(2)}, u32[]{:S(2)}) collective-permute-start(f32[8,16,128]{2,1,0:T(8,128)S(1)} %outer.1), channel_id=1, source_target_pairs={{0,0},{4,4},{8,8},{12,12},{16,16},{20,20},{24,24},{28,28},{32,32},... | collective-permute-start | bytes 196616 | tf_op jit(solution)/shard_map/ppermute | solution.py:383
  179.6 5.5 %collective-permute-done.6 = f32[8,16,128]{2,1,0:T(8,128)S(1)} collective-permute-done((f32[8,16,128]{2,1,0:T(8,128)S(1)}, f32[8,16,128]{2,1,0:T(8,128)S(1)}, u32[]{:S(2)}, u32[]{:S(2)}) %collective-permute-start.6) | collective-permute-done | bytes 65568 | tf_op jit(solution)/shard_map/ppermute | solution.py:383
  185.2 0.6 copy.7
  (2 shorter events, 0.1 us)
Async XLA Ops:
  0.8 2.2 %copy-start = (bf16[2,8,1024,128]{3,2,1,0:T(8,128)(2,1)S(1)}, bf16[2,8,1024,128]{3,2,1,0:T(8,128)(2,1)}, u32[]{:S(2)}) copy-start(bf16[2,8,1024,128]{3,2,1,0:T(8,128)(2,1)} %x_ref.1) | copy-start | bytes 12582916
  2.9 0.7 copy-start.2
  7.5 103.3 %copy-start.1 = (f32[31]{0:T(128)S(1)}, f32[31]{0:T(128)}, u32[]{:S(2)}) copy-start(f32[31]{0:T(128)} %taps_ref.3) | copy-start | bytes 376
  114.2 21.3 %collective-permute-start.2 = (bf16[8,3,128,128]{3,2,1,0:T(8,128)(2,1)S(1)}, bf16[8,3,128,128]{3,2,1,0:T(8,128)(2,1)S(1)}, u32[]{:S(2)}, u32[]{:S(2)}) collective-permute-start(bf16[8,3,128,128]{3,2,1,0:T(8,128)(2,1)S(1)} %get-tuple-element.19), channel_id=1, source_target_pairs={{0,4},{4,8},{8,12},{12,16},{16,20},{20,24},{24,28},{28,32},{32,36}... | collective-permute-start | bytes 2359304 | tf_op jit(solution)/shard_map/ppermute | solution.py:368
  117.9 36.6 %collective-permute-start.3 = (bf16[8,3,128,128]{3,2,1,0:T(8,128)(2,1)S(1)}, bf16[8,3,128,128]{3,2,1,0:T(8,128)(2,1)S(1)}, u32[]{:S(2)}, u32[]{:S(2)}) collective-permute-start(bf16[8,3,128,128]{3,2,1,0:T(8,128)(2,1)S(1)} %get-tuple-element.20), channel_id=1, source_target_pairs={{4,0},{8,4},{12,8},{16,12},{20,16},{24,20},{28,24},{32,28},{36,32}... | collective-permute-start | bytes 2359304 | tf_op jit(solution)/shard_map/ppermute | solution.py:368
  123.9 38.3 %collective-permute-start = (bf16[3,16,128,128]{3,2,1,0:T(8,128)(2,1)S(1)}, bf16[3,16,128,128]{3,2,1,0:T(8,128)(2,1)S(1)}, u32[]{:S(2)}, u32[]{:S(2)}) collective-permute-start(bf16[3,16,128,128]{3,2,1,0:T(8,128)(2,1)S(1)} %get-tuple-element.15), channel_id=1, source_target_pairs={{0,1},{1,2},{2,3},{4,5},{5,6},{6,7},{8,9},{9,10},{10,11},{12,13},{... | collective-permute-start | bytes 4718600 | tf_op jit(solution)/shard_map/ppermute | solution.py:368
  133.5 32.3 %collective-permute-start.1 = (bf16[3,16,128,128]{3,2,1,0:T(8,128)(2,1)S(1)}, bf16[3,16,128,128]{3,2,1,0:T(8,128)(2,1)S(1)}, u32[]{:S(2)}, u32[]{:S(2)}) collective-permute-start(bf16[3,16,128,128]{3,2,1,0:T(8,128)(2,1)S(1)} %get-tuple-element.16), channel_id=1, source_target_pairs={{1,0},{2,1},{3,2},{5,4},{6,5},{7,6},{9,8},{10,9},{11,10},{13,12},{... | collective-permute-start | bytes 4718600 | tf_op jit(solution)/shard_map/ppermute | solution.py:368
  154.6 19.6 %collective-permute-start.4 = (bf16[3,6,128,128]{3,2,1,0:T(8,128)(2,1)S(1)}, bf16[3,6,128,128]{3,2,1,0:T(8,128)(2,1)S(1)}, u32[]{:S(2)}, u32[]{:S(2)}) collective-permute-start(bf16[3,6,128,128]{3,2,1,0:T(8,128)(2,1)S(1)} %pad_maximum_fusion), channel_id=1, source_target_pairs={{0,1},{1,2},{2,3},{4,5},{5,6},{6,7},{8,9},{9,10},{10,11},{12,13},{... | collective-permute-start | bytes 1769480 | tf_op jit(solution)/shard_map/ppermute | solution.py:368
  156.6 17.6 %collective-permute-start.5 = (bf16[3,6,128,128]{3,2,1,0:T(8,128)(2,1)S(1)}, bf16[3,6,128,128]{3,2,1,0:T(8,128)(2,1)S(1)}, u32[]{:S(2)}, u32[]{:S(2)}) collective-permute-start(bf16[3,6,128,128]{3,2,1,0:T(8,128)(2,1)S(1)} %pad_maximum_fusion.1), channel_id=1, source_target_pairs={{1,0},{2,1},{3,2},{5,4},{6,5},{7,6},{9,8},{10,9},{11,10},{13,12},{... | collective-permute-start | bytes 1769480 | tf_op jit(solution)/shard_map/ppermute | solution.py:368
  176.9 8.3 %collective-permute-start.6 = (f32[8,16,128]{2,1,0:T(8,128)S(1)}, f32[8,16,128]{2,1,0:T(8,128)S(1)}, u32[]{:S(2)}, u32[]{:S(2)}) collective-permute-start(f32[8,16,128]{2,1,0:T(8,128)S(1)} %outer.1), channel_id=1, source_target_pairs={{0,0},{4,4},{8,8},{12,12},{16,16},{20,20},{24,24},{28,28},{32,32},... | collective-permute-start | bytes 196616 | tf_op jit(solution)/shard_map/ppermute | solution.py:383

commit v3 on v2

--- a/solution.py
+++ b/solution.py
@@ -119,8 +119,8 @@
     @pl.loop(0, cells // tile)
     def _(step):
         at = pl.multiple_of(step * tile, tile)
-        rows[:, :tile] = x_ref[:, part, pl.ds(at, tile)].astype(jnp.float32)
-        flat = rows.reshape(frames * PITCH, width)
+        rows[:frames, :tile] = x_ref[:, part, pl.ds(at, tile)].astype(jnp.float32)
+        flat = rows.reshape((frames + 1) * PITCH, width)
         weights = matrix[...]
         for cell in range(tile):
             values = flat[pl.ds(cell, frames, stride=PITCH), :]
@@ -159,7 +159,7 @@
         in_specs=[pl.BlockSpec(memory_space=pltpu.SMEM), vmem] + [vmem] * len(before),
         out_specs=[vmem] * 3,
         out_shape=[shape(planes, 8), halo, halo],
-        scratch_shapes=[pltpu.VMEM((frames, frames), jnp.bfloat16), pltpu.VMEM((frames, PITCH, width), jnp.float32)],
+        scratch_shapes=[pltpu.VMEM((frames, frames), jnp.bfloat16), pltpu.VMEM((frames + 1, PITCH, width), jnp.float32)],
         cost_estimate=COST,
         compiler_params=params(),
         name="filter",

time: 186 us -> 186 us (level)
  no operation moved by 1% of the time
where the time goes in v3:
time: 186 us
  blocking collectives  103 us (55%)
  starting transfers between devices  28.1 us (15%)
  waiting for transfers between devices  28.1 us (15%)
  Pallas kernels  21.8 us (12%)
  local copies, waits for them, and re-layouts  4.32 us (2%)
    all_to_all x1, blocking collectives, body(): arrived = lax.all_to_all(sent, 'frames', 0, 0)  103 us
    ppermute x6, starting transfers between devices, shift(): lax.ppermute(array, axis, [(p, places[i + by]) for i, p in enumerate(plac...  25.3 us
    ppermute x6, waiting for transfers between devices, shift(): lax.ppermute(array, axis, [(p, places[i + by]) for i, p in enumerate(plac...  22.6 us
    pallas_call x1, Pallas kernels, inner(): pl.pallas_call(inner_kernel, in_specs=[vmem] * 4, out_specs=[vmem] * 2, o...  8.27 us
    pallas_call x2, Pallas kernels, filter_cells(): pl.pallas_call(functools.partial(filter_kernel, part), in_specs=[pl.Block...  6.89 us
    ppermute x1, waiting for transfers between devices, body(): return lax.ppermute(image, 'frames', [(p, t) for t, p in enumerate(slots)])  5.54 us
    unnamed x8, local copies, waits for them, and re-layouts  4.23 us
    pallas_call x1, Pallas kernels, register(): pl.pallas_call(functools.partial(register_kernel, slots), grid=(frames, p...  3.95 us
  transfers between devices with their start and end apart: 7, of which 3 were waited for; matrix products, arithmetic and copies ran while one was open for 0% of the time, Pallas kernels for 6%

profile of v3, /device:TPU:65, one launch (start us, length us, event | category | flops | bytes accessed | tf_op | source)
XLA Modules:
  0.0 185.9 jit_solution(17894789938007242795)
XLA Ops:
  0.0 0.8 copy.5.shifts_ref
  0.8 0.0 copy-start
  0.8 2.2 %copy-done = bf16[2,8,1024,128]{3,2,1,0:T(8,128)(2,1)S(1)} copy-done((bf16[2,8,1024,128]{3,2,1,0:T(8,128)(2,1)S(1)}, bf16[2,8,1024,128]{3,2,1,0:T(8,128)(2,1)}, u32[]{:S(2)}) %copy-start) | copy-done | bytes 4194328
  2.9 0.0 copy-start.2
  2.9 0.7 copy-done.2
  3.6 4.0 %register.1 = bf16[64,2,2,64,128]{4,3,2,1,0:T(8,128)(2,1)S(1)} custom-call(s32[1]{0:T(128)} %bitcast.first_ref, s32[128]{0:T(128)S(1)} %copy-done.2, f32[16,2]{1,0:T(8,128)S(1)} %copy.5.shifts_ref, bf16[2,8,1024,128]{3,2,1,0:T(8,128)(2,1)S(1)} %copy-done), custom_call_target="tpu_custom_call" | custom-call | flops 1 | bytes 1 | tf_op jit(solution)/shard_map/register/pallas_call | solution.py:91
  7.6 0.0 copy-start.1
  7.6 103.2 %all_to_all.5 = bf16[64,2,2,64,128]{4,3,2,1,0:T(8,128)(2,1)S(1)} all-to-all(bf16[64,2,2,64,128]{4,3,2,1,0:T(8,128)(2,1)S(1)} %register.1), channel_id=1, replica_groups=mesh['frames'=64,'gz'=4] {'frames'}, dimensions={0} | all-to-all | bytes 8388608 | tf_op jit(solution)/shard_map/all_to_all | solution.py:371
  110.8 0.0 copy-done.1
  110.8 3.4 %filter.2 = (bf16[8,8,128,128]{3,2,1,0:T(8,128)(2,1)S(1)}, bf16[8,3,128,128]{3,2,1,0:T(8,128)(2,1)S(1)}, bf16[8,3,128,128]{3,2,1,0:T(8,128)(2,1)S(1)}) custom-call(f32[31]{0:T(128)S(1)} %copy-done.1, bf16[128,2,64,128]{3,2,1,0:T(8,128)(2,1)S(1)} %bitcast.2), custom_call_target="tpu_custom_call" | custom-call | flops 1 | bytes 1 | tf_op jit(solution)/shard_map/filter/pallas_call | solution.py:157
  114.2 3.7 %collective-permute-start.2 = (bf16[8,3,128,128]{3,2,1,0:T(8,128)(2,1)S(1)}, bf16[8,3,128,128]{3,2,1,0:T(8,128)(2,1)S(1)}, u32[]{:S(2)}, u32[]{:S(2)}) collective-permute-start(bf16[8,3,128,128]{3,2,1,0:T(8,128)(2,1)S(1)} %get-tuple-element.19), channel_id=1, source_target_pairs={{0,4},{4,8},{8,12},{12,16},{16,20},{20,24},{24,28},{28,32},{32,36}... | collective-permute-start | bytes 2359304 | tf_op jit(solution)/shard_map/ppermute | solution.py:368
  117.9 2.5 %collective-permute-start.3 = (bf16[8,3,128,128]{3,2,1,0:T(8,128)(2,1)S(1)}, bf16[8,3,128,128]{3,2,1,0:T(8,128)(2,1)S(1)}, u32[]{:S(2)}, u32[]{:S(2)}) collective-permute-start(bf16[8,3,128,128]{3,2,1,0:T(8,128)(2,1)S(1)} %get-tuple-element.20), channel_id=1, source_target_pairs={{4,0},{8,4},{12,8},{16,12},{20,16},{24,20},{28,24},{32,28},{36,32}... | collective-permute-start | bytes 2359304 | tf_op jit(solution)/shard_map/ppermute | solution.py:368
  120.4 3.5 %filter.3 = (bf16[8,8,128,128]{3,2,1,0:T(8,128)(2,1)S(1)}, bf16[3,16,128,128]{3,2,1,0:T(8,128)(2,1)S(1)}, bf16[3,16,128,128]{3,2,1,0:T(8,128)(2,1)S(1)}) custom-call(f32[31]{0:T(128)S(1)} %copy-done.1, bf16[128,2,64,128]{3,2,1,0:T(8,128)(2,1)S(1)} %bitcast.3, bf16[8,8,128,128]{3,2,1,0:T(8,128)(2,1)S(1)} %get-tuple-element.13.refs_0_.ends), custom_call_target="tpu_custom_call" | custom-call | flops 1 | bytes 1 | tf_op jit(solution)/shard_map/filter/pallas_call | solution.py:157
  124.0 9.6 %collective-permute-start = (bf16[3,16,128,128]{3,2,1,0:T(8,128)(2,1)S(1)}, bf16[3,16,128,128]{3,2,1,0:T(8,128)(2,1)S(1)}, u32[]{:S(2)}, u32[]{:S(2)}) collective-permute-start(bf16[3,16,128,128]{3,2,1,0:T(8,128)(2,1)S(1)} %get-tuple-element.15), channel_id=1, source_target_pairs={{0,1},{1,2},{2,3},{4,5},{5,6},{6,7},{8,9},{9,10},{10,11},{12,13},{... | collective-permute-start | bytes 4718600 | tf_op jit(solution)/shard_map/ppermute | solution.py:368
  133.6 1.9 %collective-permute-start.1 = (bf16[3,16,128,128]{3,2,1,0:T(8,128)(2,1)S(1)}, bf16[3,16,128,128]{3,2,1,0:T(8,128)(2,1)S(1)}, u32[]{:S(2)}, u32[]{:S(2)}) collective-permute-start(bf16[3,16,128,128]{3,2,1,0:T(8,128)(2,1)S(1)} %get-tuple-element.16), channel_id=1, source_target_pairs={{1,0},{2,1},{3,2},{5,4},{6,5},{7,6},{9,8},{10,9},{11,10},{13,12},{... | collective-permute-start | bytes 4718600 | tf_op jit(solution)/shard_map/ppermute | solution.py:368
  135.5 0.0 collective-permute-done.2.refs_0_
  135.6 18.9 %collective-permute-done.3.refs_1_ = bf16[8,3,128,128]{3,2,1,0:T(8,128)(2,1)S(1)} collective-permute-done((bf16[8,3,128,128]{3,2,1,0:T(8,128)(2,1)S(1)}, bf16[8,3,128,128]{3,2,1,0:T(8,128)(2,1)S(1)}, u32[]{:S(2)}, u32[]{:S(2)}) %collective-permute-start.3) | collective-permute-done | bytes 786464 | tf_op jit(solution)/shard_map/ppermute | solution.py:368
  154.6 0.1 pad_maximum_fusion
  154.6 1.9 %collective-permute-start.4 = (bf16[3,6,128,128]{3,2,1,0:T(8,128)(2,1)S(1)}, bf16[3,6,128,128]{3,2,1,0:T(8,128)(2,1)S(1)}, u32[]{:S(2)}, u32[]{:S(2)}) collective-permute-start(bf16[3,6,128,128]{3,2,1,0:T(8,128)(2,1)S(1)} %pad_maximum_fusion), channel_id=1, source_target_pairs={{0,1},{1,2},{2,3},{4,5},{5,6},{6,7},{8,9},{9,10},{10,11},{12,13},{... | collective-permute-start | bytes 1769480 | tf_op jit(solution)/shard_map/ppermute | solution.py:368
  156.5 0.1 pad_maximum_fusion.1
  156.6 5.7 %collective-permute-start.5 = (bf16[3,6,128,128]{3,2,1,0:T(8,128)(2,1)S(1)}, bf16[3,6,128,128]{3,2,1,0:T(8,128)(2,1)S(1)}, u32[]{:S(2)}, u32[]{:S(2)}) collective-permute-start(bf16[3,6,128,128]{3,2,1,0:T(8,128)(2,1)S(1)} %pad_maximum_fusion.1), channel_id=1, source_target_pairs={{1,0},{2,1},{3,2},{5,4},{6,5},{7,6},{9,8},{10,9},{11,10},{13,12},{... | collective-permute-start | bytes 1769480 | tf_op jit(solution)/shard_map/ppermute | solution.py:368
  162.3 0.0 collective-permute-done.low
  162.3 3.7 %collective-permute-done.1.high = bf16[3,16,128,128]{3,2,1,0:T(8,128)(2,1)S(1)} collective-permute-done((bf16[3,16,128,128]{3,2,1,0:T(8,128)(2,1)S(1)}, bf16[3,16,128,128]{3,2,1,0:T(8,128)(2,1)S(1)}, u32[]{:S(2)}, u32[]{:S(2)}) %collective-permute-start.1) | collective-permute-done | bytes 1572896 | tf_op jit(solution)/shard_map/ppermute | solution.py:368
  165.9 8.3 %inner.1 = (f32[8,16,128]{2,1,0:T(8,128)S(1)}, f32[6,8,128,128]{3,2,1,0:T(8,128)S(1)}) custom-call(bf16[8,8,128,128]{3,2,1,0:T(8,128)(2,1)S(1)} %get-tuple-element.13.refs_0_.ends, bf16[8,8,128,128]{3,2,1,0:T(8,128)(2,1)S(1)} %get-tuple-element.14.middle, bf16[3,16,128,128]{3,2,1,0:T(8,128)(2,1)S(1)} %collective-permute-done.low, ...), custom_call_target="tpu_custom_call" | custom-call | flops 1 | bytes 1 | tf_op jit(solution)/shard_map/inner/pallas_call | solution.py:320
  174.2 0.0 collective-permute-done.4.refs_2_
  174.2 0.0 collective-permute-done.5.refs_3_
  174.2 2.7 %outer.1 = f32[8,16,128]{2,1,0:T(8,128)S(1)} custom-call(bf16[8,8,128,128]{3,2,1,0:T(8,128)(2,1)S(1)} %get-tuple-element.13.refs_0_.ends, f32[6,8,128,128]{3,2,1,0:T(8,128)S(1)} %get-tuple-element.17.part, f32[8,16,128]{2,1,0:T(8,128)S(1)} %get-tuple-element.18.image, bf16[8,3,128,128]{3,2,1,0:T(8,128)(2,1)S(1)} %collective-permute-done.2.refs_0_, ...), custom_call_target="tpu_custom_call" | custom-call | flops 1 | bytes 1 | tf_op jit(solution)/shard_map/outer/pallas_call | solution.py:342
  176.9 2.8 %collective-permute-start.6 = (f32[8,16,128]{2,1,0:T(8,128)S(1)}, f32[8,16,128]{2,1,0:T(8,128)S(1)}, u32[]{:S(2)}, u32[]{:S(2)}) collective-permute-start(f32[8,16,128]{2,1,0:T(8,128)S(1)} %outer.1), channel_id=1, source_target_pairs={{0,0},{4,4},{8,8},{12,12},{16,16},{20,20},{24,24},{28,28},{32,32},... | collective-permute-start | bytes 196616 | tf_op jit(solution)/shard_map/ppermute | solution.py:383
  179.7 5.5 %collective-permute-done.6 = f32[8,16,128]{2,1,0:T(8,128)S(1)} collective-permute-done((f32[8,16,128]{2,1,0:T(8,128)S(1)}, f32[8,16,128]{2,1,0:T(8,128)S(1)}, u32[]{:S(2)}, u32[]{:S(2)}) %collective-permute-start.6) | collective-permute-done | bytes 65568 | tf_op jit(solution)/shard_map/ppermute | solution.py:383
  185.2 0.6 copy.7
  (2 shorter events, 0.1 us)
Async XLA Ops:
  0.8 2.2 %copy-start = (bf16[2,8,1024,128]{3,2,1,0:T(8,128)(2,1)S(1)}, bf16[2,8,1024,128]{3,2,1,0:T(8,128)(2,1)}, u32[]{:S(2)}) copy-start(bf16[2,8,1024,128]{3,2,1,0:T(8,128)(2,1)} %x_ref.1) | copy-start | bytes 12582916
  2.9 0.7 copy-start.2
  7.6 103.3 %copy-start.1 = (f32[31]{0:T(128)S(1)}, f32[31]{0:T(128)}, u32[]{:S(2)}) copy-start(f32[31]{0:T(128)} %taps_ref.3) | copy-start | bytes 376
  114.2 21.3 %collective-permute-start.2 = (bf16[8,3,128,128]{3,2,1,0:T(8,128)(2,1)S(1)}, bf16[8,3,128,128]{3,2,1,0:T(8,128)(2,1)S(1)}, u32[]{:S(2)}, u32[]{:S(2)}) collective-permute-start(bf16[8,3,128,128]{3,2,1,0:T(8,128)(2,1)S(1)} %get-tuple-element.19), channel_id=1, source_target_pairs={{0,4},{4,8},{8,12},{12,16},{16,20},{20,24},{24,28},{28,32},{32,36}... | collective-permute-start | bytes 2359304 | tf_op jit(solution)/shard_map/ppermute | solution.py:368
  117.9 36.6 %collective-permute-start.3 = (bf16[8,3,128,128]{3,2,1,0:T(8,128)(2,1)S(1)}, bf16[8,3,128,128]{3,2,1,0:T(8,128)(2,1)S(1)}, u32[]{:S(2)}, u32[]{:S(2)}) collective-permute-start(bf16[8,3,128,128]{3,2,1,0:T(8,128)(2,1)S(1)} %get-tuple-element.20), channel_id=1, source_target_pairs={{4,0},{8,4},{12,8},{16,12},{20,16},{24,20},{28,24},{32,28},{36,32}... | collective-permute-start | bytes 2359304 | tf_op jit(solution)/shard_map/ppermute | solution.py:368
  124.0 38.3 %collective-permute-start = (bf16[3,16,128,128]{3,2,1,0:T(8,128)(2,1)S(1)}, bf16[3,16,128,128]{3,2,1,0:T(8,128)(2,1)S(1)}, u32[]{:S(2)}, u32[]{:S(2)}) collective-permute-start(bf16[3,16,128,128]{3,2,1,0:T(8,128)(2,1)S(1)} %get-tuple-element.15), channel_id=1, source_target_pairs={{0,1},{1,2},{2,3},{4,5},{5,6},{6,7},{8,9},{9,10},{10,11},{12,13},{... | collective-permute-start | bytes 4718600 | tf_op jit(solution)/shard_map/ppermute | solution.py:368
  133.6 32.4 %collective-permute-start.1 = (bf16[3,16,128,128]{3,2,1,0:T(8,128)(2,1)S(1)}, bf16[3,16,128,128]{3,2,1,0:T(8,128)(2,1)S(1)}, u32[]{:S(2)}, u32[]{:S(2)}) collective-permute-start(bf16[3,16,128,128]{3,2,1,0:T(8,128)(2,1)S(1)} %get-tuple-element.16), channel_id=1, source_target_pairs={{1,0},{2,1},{3,2},{5,4},{6,5},{7,6},{9,8},{10,9},{11,10},{13,12},{... | collective-permute-start | bytes 4718600 | tf_op jit(solution)/shard_map/ppermute | solution.py:368
  154.6 19.6 %collective-permute-start.4 = (bf16[3,6,128,128]{3,2,1,0:T(8,128)(2,1)S(1)}, bf16[3,6,128,128]{3,2,1,0:T(8,128)(2,1)S(1)}, u32[]{:S(2)}, u32[]{:S(2)}) collective-permute-start(bf16[3,6,128,128]{3,2,1,0:T(8,128)(2,1)S(1)} %pad_maximum_fusion), channel_id=1, source_target_pairs={{0,1},{1,2},{2,3},{4,5},{5,6},{6,7},{8,9},{9,10},{10,11},{12,13},{... | collective-permute-start | bytes 1769480 | tf_op jit(solution)/shard_map/ppermute | solution.py:368
  156.6 17.6 %collective-permute-start.5 = (bf16[3,6,128,128]{3,2,1,0:T(8,128)(2,1)S(1)}, bf16[3,6,128,128]{3,2,1,0:T(8,128)(2,1)S(1)}, u32[]{:S(2)}, u32[]{:S(2)}) collective-permute-start(bf16[3,6,128,128]{3,2,1,0:T(8,128)(2,1)S(1)} %pad_maximum_fusion.1), channel_id=1, source_target_pairs={{1,0},{2,1},{3,2},{5,4},{6,5},{7,6},{9,8},{10,9},{11,10},{13,12},{... | collective-permute-start | bytes 1769480 | tf_op jit(solution)/shard_map/ppermute | solution.py:368
  176.9 8.3 %collective-permute-start.6 = (f32[8,16,128]{2,1,0:T(8,128)S(1)}, f32[8,16,128]{2,1,0:T(8,128)S(1)}, u32[]{:S(2)}, u32[]{:S(2)}) collective-permute-start(f32[8,16,128]{2,1,0:T(8,128)S(1)} %outer.1), channel_id=1, source_target_pairs={{0,0},{4,4},{8,8},{12,12},{16,16},{20,20},{24,24},{28,28},{32,32},... | collective-permute-start | bytes 196616 | tf_op jit(solution)/shard_map/ppermute | solution.py:383

commit v4 on v3

--- a/solution.py
+++ b/solution.py
@@ -123,9 +123,12 @@
         flat = rows.reshape((frames + 1) * PITCH, width)
         weights = matrix[...]
         for cell in range(tile):
-            values = flat[pl.ds(cell, frames, stride=PITCH), :]
-            baseline = jnp.dot(weights, values.astype(jnp.bfloat16), preferred_element_type=jnp.float32)
-            detrended = values - baseline
+            if cell % 2 == 0:
+                two = [flat[pl.ds(cell + k, frames, stride=PITCH), :] for k in range(2)]
+                wide = jnp.concatenate([values.astype(jnp.bfloat16) for values in two], axis=1)
+                wide = jnp.dot(weights, wide, preferred_element_type=jnp.float32)
+            side = cell % 2
+            detrended = two[side] - wide[:, side * width : (side + 1) * width]
             average = jnp.sum(detrended, axis=0, keepdims=True) * (1.0 / frames)
             centred = detrended - average
             power = jnp.sum(centred * centred, axis=0, keepdims=True) * (1.0 / frames)

time: 186 us -> 186 us (level)
  no operation moved by 1% of the time
where the time goes in v4:
time: 186 us
  blocking collectives  103 us (55%)
  starting transfers between devices  28.1 us (15%)
  waiting for transfers between devices  28.1 us (15%)
  Pallas kernels  21.8 us (12%)
  local copies, waits for them, and re-layouts  4.32 us (2%)
    all_to_all x1, blocking collectives, body(): arrived = lax.all_to_all(sent, 'frames', 0, 0)  103 us
    ppermute x6, starting transfers between devices, shift(): lax.ppermute(array, axis, [(p, places[i + by]) for i, p in enumerate(plac...  25.3 us
    ppermute x6, waiting for transfers between devices, shift(): lax.ppermute(array, axis, [(p, places[i + by]) for i, p in enumerate(plac...  22.6 us
    pallas_call x1, Pallas kernels, inner(): pl.pallas_call(inner_kernel, in_specs=[vmem] * 4, out_specs=[vmem] * 2, o...  8.27 us
    pallas_call x2, Pallas kernels, filter_cells(): pl.pallas_call(functools.partial(filter_kernel, part), in_specs=[pl.Block...  6.93 us
    ppermute x1, waiting for transfers between devices, body(): return lax.ppermute(image, 'frames', [(p, t) for t, p in enumerate(slots)])  5.54 us
    unnamed x8, local copies, waits for them, and re-layouts  4.23 us
    pallas_call x1, Pallas kernels, register(): pl.pallas_call(functools.partial(register_kernel, slots), grid=(frames, p...  3.95 us
  transfers between devices with their start and end apart: 7, of which 3 were waited for; matrix products, arithmetic and copies ran while one was open for 0% of the time, Pallas kernels for 6%

profile of v4, /device:TPU:65, one launch (start us, length us, event | category | flops | bytes accessed | tf_op | source)
XLA Modules:
  0.0 185.9 jit_solution(1330813583714399005)
XLA Ops:
  0.0 0.8 copy.5.shifts_ref
  0.8 0.0 copy-start
  0.8 2.2 %copy-done = bf16[2,8,1024,128]{3,2,1,0:T(8,128)(2,1)S(1)} copy-done((bf16[2,8,1024,128]{3,2,1,0:T(8,128)(2,1)S(1)}, bf16[2,8,1024,128]{3,2,1,0:T(8,128)(2,1)}, u32[]{:S(2)}) %copy-start) | copy-done | bytes 4194328
  2.9 0.0 copy-start.2
  2.9 0.7 copy-done.2
  3.6 4.0 %register.1 = bf16[64,2,2,64,128]{4,3,2,1,0:T(8,128)(2,1)S(1)} custom-call(s32[1]{0:T(128)} %bitcast.first_ref, s32[128]{0:T(128)S(1)} %copy-done.2, f32[16,2]{1,0:T(8,128)S(1)} %copy.5.shifts_ref, bf16[2,8,1024,128]{3,2,1,0:T(8,128)(2,1)S(1)} %copy-done), custom_call_target="tpu_custom_call" | custom-call | flops 1 | bytes 1 | tf_op jit(solution)/shard_map/register/pallas_call | solution.py:91
  7.6 0.0 copy-start.1
  7.6 103.3 %all_to_all.5 = bf16[64,2,2,64,128]{4,3,2,1,0:T(8,128)(2,1)S(1)} all-to-all(bf16[64,2,2,64,128]{4,3,2,1,0:T(8,128)(2,1)S(1)} %register.1), channel_id=1, replica_groups=mesh['frames'=64,'gz'=4] {'frames'}, dimensions={0} | all-to-all | bytes 8388608 | tf_op jit(solution)/shard_map/all_to_all | solution.py:374
  110.8 0.0 copy-done.1
  110.8 3.4 %filter.2 = (bf16[8,8,128,128]{3,2,1,0:T(8,128)(2,1)S(1)}, bf16[8,3,128,128]{3,2,1,0:T(8,128)(2,1)S(1)}, bf16[8,3,128,128]{3,2,1,0:T(8,128)(2,1)S(1)}) custom-call(f32[31]{0:T(128)S(1)} %copy-done.1, bf16[128,2,64,128]{3,2,1,0:T(8,128)(2,1)S(1)} %bitcast.2), custom_call_target="tpu_custom_call" | custom-call | flops 1 | bytes 1 | tf_op jit(solution)/shard_map/filter/pallas_call | solution.py:160
  114.2 3.7 %collective-permute-start.2 = (bf16[8,3,128,128]{3,2,1,0:T(8,128)(2,1)S(1)}, bf16[8,3,128,128]{3,2,1,0:T(8,128)(2,1)S(1)}, u32[]{:S(2)}, u32[]{:S(2)}) collective-permute-start(bf16[8,3,128,128]{3,2,1,0:T(8,128)(2,1)S(1)} %get-tuple-element.19), channel_id=1, source_target_pairs={{0,4},{4,8},{8,12},{12,16},{16,20},{20,24},{24,28},{28,32},{32,36}... | collective-permute-start | bytes 2359304 | tf_op jit(solution)/shard_map/ppermute | solution.py:371
  118.0 2.5 %collective-permute-start.3 = (bf16[8,3,128,128]{3,2,1,0:T(8,128)(2,1)S(1)}, bf16[8,3,128,128]{3,2,1,0:T(8,128)(2,1)S(1)}, u32[]{:S(2)}, u32[]{:S(2)}) collective-permute-start(bf16[8,3,128,128]{3,2,1,0:T(8,128)(2,1)S(1)} %get-tuple-element.20), channel_id=1, source_target_pairs={{4,0},{8,4},{12,8},{16,12},{20,16},{24,20},{28,24},{32,28},{36,32}... | collective-permute-start | bytes 2359304 | tf_op jit(solution)/shard_map/ppermute | solution.py:371
  120.5 3.5 %filter.3 = (bf16[8,8,128,128]{3,2,1,0:T(8,128)(2,1)S(1)}, bf16[3,16,128,128]{3,2,1,0:T(8,128)(2,1)S(1)}, bf16[3,16,128,128]{3,2,1,0:T(8,128)(2,1)S(1)}) custom-call(f32[31]{0:T(128)S(1)} %copy-done.1, bf16[128,2,64,128]{3,2,1,0:T(8,128)(2,1)S(1)} %bitcast.3, bf16[8,8,128,128]{3,2,1,0:T(8,128)(2,1)S(1)} %get-tuple-element.13.refs_0_.ends), custom_call_target="tpu_custom_call" | custom-call | flops 1 | bytes 1 | tf_op jit(solution)/shard_map/filter/pallas_call | solution.py:160
  124.0 9.6 %collective-permute-start = (bf16[3,16,128,128]{3,2,1,0:T(8,128)(2,1)S(1)}, bf16[3,16,128,128]{3,2,1,0:T(8,128)(2,1)S(1)}, u32[]{:S(2)}, u32[]{:S(2)}) collective-permute-start(bf16[3,16,128,128]{3,2,1,0:T(8,128)(2,1)S(1)} %get-tuple-element.15), channel_id=1, source_target_pairs={{0,1},{1,2},{2,3},{4,5},{5,6},{6,7},{8,9},{9,10},{10,11},{12,13},{... | collective-permute-start | bytes 4718600 | tf_op jit(solution)/shard_map/ppermute | solution.py:371
  133.6 1.9 %collective-permute-start.1 = (bf16[3,16,128,128]{3,2,1,0:T(8,128)(2,1)S(1)}, bf16[3,16,128,128]{3,2,1,0:T(8,128)(2,1)S(1)}, u32[]{:S(2)}, u32[]{:S(2)}) collective-permute-start(bf16[3,16,128,128]{3,2,1,0:T(8,128)(2,1)S(1)} %get-tuple-element.16), channel_id=1, source_target_pairs={{1,0},{2,1},{3,2},{5,4},{6,5},{7,6},{9,8},{10,9},{11,10},{13,12},{... | collective-permute-start | bytes 4718600 | tf_op jit(solution)/shard_map/ppermute | solution.py:371
  135.6 0.0 collective-permute-done.2.refs_0_
  135.6 18.9 %collective-permute-done.3.refs_1_ = bf16[8,3,128,128]{3,2,1,0:T(8,128)(2,1)S(1)} collective-permute-done((bf16[8,3,128,128]{3,2,1,0:T(8,128)(2,1)S(1)}, bf16[8,3,128,128]{3,2,1,0:T(8,128)(2,1)S(1)}, u32[]{:S(2)}, u32[]{:S(2)}) %collective-permute-start.3) | collective-permute-done | bytes 786464 | tf_op jit(solution)/shard_map/ppermute | solution.py:371
  154.6 0.1 pad_maximum_fusion
  154.6 1.9 %collective-permute-start.4 = (bf16[3,6,128,128]{3,2,1,0:T(8,128)(2,1)S(1)}, bf16[3,6,128,128]{3,2,1,0:T(8,128)(2,1)S(1)}, u32[]{:S(2)}, u32[]{:S(2)}) collective-permute-start(bf16[3,6,128,128]{3,2,1,0:T(8,128)(2,1)S(1)} %pad_maximum_fusion), channel_id=1, source_target_pairs={{0,1},{1,2},{2,3},{4,5},{5,6},{6,7},{8,9},{9,10},{10,11},{12,13},{... | collective-permute-start | bytes 1769480 | tf_op jit(solution)/shard_map/ppermute | solution.py:371
  156.6 0.1 pad_maximum_fusion.1
  156.6 5.7 %collective-permute-start.5 = (bf16[3,6,128,128]{3,2,1,0:T(8,128)(2,1)S(1)}, bf16[3,6,128,128]{3,2,1,0:T(8,128)(2,1)S(1)}, u32[]{:S(2)}, u32[]{:S(2)}) collective-permute-start(bf16[3,6,128,128]{3,2,1,0:T(8,128)(2,1)S(1)} %pad_maximum_fusion.1), channel_id=1, source_target_pairs={{1,0},{2,1},{3,2},{5,4},{6,5},{7,6},{9,8},{10,9},{11,10},{13,12},{... | collective-permute-start | bytes 1769480 | tf_op jit(solution)/shard_map/ppermute | solution.py:371
  162.3 0.0 collective-permute-done.low
  162.3 3.7 %collective-permute-done.1.high = bf16[3,16,128,128]{3,2,1,0:T(8,128)(2,1)S(1)} collective-permute-done((bf16[3,16,128,128]{3,2,1,0:T(8,128)(2,1)S(1)}, bf16[3,16,128,128]{3,2,1,0:T(8,128)(2,1)S(1)}, u32[]{:S(2)}, u32[]{:S(2)}) %collective-permute-start.1) | collective-permute-done | bytes 1572896 | tf_op jit(solution)/shard_map/ppermute | solution.py:371
  166.0 8.3 %inner.1 = (f32[8,16,128]{2,1,0:T(8,128)S(1)}, f32[6,8,128,128]{3,2,1,0:T(8,128)S(1)}) custom-call(bf16[8,8,128,128]{3,2,1,0:T(8,128)(2,1)S(1)} %get-tuple-element.13.refs_0_.ends, bf16[8,8,128,128]{3,2,1,0:T(8,128)(2,1)S(1)} %get-tuple-element.14.middle, bf16[3,16,128,128]{3,2,1,0:T(8,128)(2,1)S(1)} %collective-permute-done.low, ...), custom_call_target="tpu_custom_call" | custom-call | flops 1 | bytes 1 | tf_op jit(solution)/shard_map/inner/pallas_call | solution.py:323
  174.3 0.0 collective-permute-done.4.refs_2_
  174.3 0.0 collective-permute-done.5.refs_3_
  174.3 2.7 %outer.1 = f32[8,16,128]{2,1,0:T(8,128)S(1)} custom-call(bf16[8,8,128,128]{3,2,1,0:T(8,128)(2,1)S(1)} %get-tuple-element.13.refs_0_.ends, f32[6,8,128,128]{3,2,1,0:T(8,128)S(1)} %get-tuple-element.17.part, f32[8,16,128]{2,1,0:T(8,128)S(1)} %get-tuple-element.18.image, bf16[8,3,128,128]{3,2,1,0:T(8,128)(2,1)S(1)} %collective-permute-done.2.refs_0_, ...), custom_call_target="tpu_custom_call" | custom-call | flops 1 | bytes 1 | tf_op jit(solution)/shard_map/outer/pallas_call | solution.py:345
  177.0 2.8 %collective-permute-start.6 = (f32[8,16,128]{2,1,0:T(8,128)S(1)}, f32[8,16,128]{2,1,0:T(8,128)S(1)}, u32[]{:S(2)}, u32[]{:S(2)}) collective-permute-start(f32[8,16,128]{2,1,0:T(8,128)S(1)} %outer.1), channel_id=1, source_target_pairs={{0,0},{4,4},{8,8},{12,12},{16,16},{20,20},{24,24},{28,28},{32,32},... | collective-permute-start | bytes 196616 | tf_op jit(solution)/shard_map/ppermute | solution.py:386
  179.7 5.5 %collective-permute-done.6 = f32[8,16,128]{2,1,0:T(8,128)S(1)} collective-permute-done((f32[8,16,128]{2,1,0:T(8,128)S(1)}, f32[8,16,128]{2,1,0:T(8,128)S(1)}, u32[]{:S(2)}, u32[]{:S(2)}) %collective-permute-start.6) | collective-permute-done | bytes 65568 | tf_op jit(solution)/shard_map/ppermute | solution.py:386
  185.3 0.6 copy.7
  (2 shorter events, 0.1 us)
Async XLA Ops:
  0.8 2.2 %copy-start = (bf16[2,8,1024,128]{3,2,1,0:T(8,128)(2,1)S(1)}, bf16[2,8,1024,128]{3,2,1,0:T(8,128)(2,1)}, u32[]{:S(2)}) copy-start(bf16[2,8,1024,128]{3,2,1,0:T(8,128)(2,1)} %x_ref.1) | copy-start | bytes 12582916
  2.9 0.7 copy-start.2
  7.6 103.3 %copy-start.1 = (f32[31]{0:T(128)S(1)}, f32[31]{0:T(128)}, u32[]{:S(2)}) copy-start(f32[31]{0:T(128)} %taps_ref.3) | copy-start | bytes 376
  114.2 21.3 %collective-permute-start.2 = (bf16[8,3,128,128]{3,2,1,0:T(8,128)(2,1)S(1)}, bf16[8,3,128,128]{3,2,1,0:T(8,128)(2,1)S(1)}, u32[]{:S(2)}, u32[]{:S(2)}) collective-permute-start(bf16[8,3,128,128]{3,2,1,0:T(8,128)(2,1)S(1)} %get-tuple-element.19), channel_id=1, source_target_pairs={{0,4},{4,8},{8,12},{12,16},{16,20},{20,24},{24,28},{28,32},{32,36}... | collective-permute-start | bytes 2359304 | tf_op jit(solution)/shard_map/ppermute | solution.py:371
  118.0 36.6 %collective-permute-start.3 = (bf16[8,3,128,128]{3,2,1,0:T(8,128)(2,1)S(1)}, bf16[8,3,128,128]{3,2,1,0:T(8,128)(2,1)S(1)}, u32[]{:S(2)}, u32[]{:S(2)}) collective-permute-start(bf16[8,3,128,128]{3,2,1,0:T(8,128)(2,1)S(1)} %get-tuple-element.20), channel_id=1, source_target_pairs={{4,0},{8,4},{12,8},{16,12},{20,16},{24,20},{28,24},{32,28},{36,32}... | collective-permute-start | bytes 2359304 | tf_op jit(solution)/shard_map/ppermute | solution.py:371
  124.0 38.3 %collective-permute-start = (bf16[3,16,128,128]{3,2,1,0:T(8,128)(2,1)S(1)}, bf16[3,16,128,128]{3,2,1,0:T(8,128)(2,1)S(1)}, u32[]{:S(2)}, u32[]{:S(2)}) collective-permute-start(bf16[3,16,128,128]{3,2,1,0:T(8,128)(2,1)S(1)} %get-tuple-element.15), channel_id=1, source_target_pairs={{0,1},{1,2},{2,3},{4,5},{5,6},{6,7},{8,9},{9,10},{10,11},{12,13},{... | collective-permute-start | bytes 4718600 | tf_op jit(solution)/shard_map/ppermute | solution.py:371
  133.6 32.3 %collective-permute-start.1 = (bf16[3,16,128,128]{3,2,1,0:T(8,128)(2,1)S(1)}, bf16[3,16,128,128]{3,2,1,0:T(8,128)(2,1)S(1)}, u32[]{:S(2)}, u32[]{:S(2)}) collective-permute-start(bf16[3,16,128,128]{3,2,1,0:T(8,128)(2,1)S(1)} %get-tuple-element.16), channel_id=1, source_target_pairs={{1,0},{2,1},{3,2},{5,4},{6,5},{7,6},{9,8},{10,9},{11,10},{13,12},{... | collective-permute-start | bytes 4718600 | tf_op jit(solution)/shard_map/ppermute | solution.py:371
  154.6 19.6 %collective-permute-start.4 = (bf16[3,6,128,128]{3,2,1,0:T(8,128)(2,1)S(1)}, bf16[3,6,128,128]{3,2,1,0:T(8,128)(2,1)S(1)}, u32[]{:S(2)}, u32[]{:S(2)}) collective-permute-start(bf16[3,6,128,128]{3,2,1,0:T(8,128)(2,1)S(1)} %pad_maximum_fusion), channel_id=1, source_target_pairs={{0,1},{1,2},{2,3},{4,5},{5,6},{6,7},{8,9},{9,10},{10,11},{12,13},{... | collective-permute-start | bytes 1769480 | tf_op jit(solution)/shard_map/ppermute | solution.py:371
  156.6 17.6 %collective-permute-start.5 = (bf16[3,6,128,128]{3,2,1,0:T(8,128)(2,1)S(1)}, bf16[3,6,128,128]{3,2,1,0:T(8,128)(2,1)S(1)}, u32[]{:S(2)}, u32[]{:S(2)}) collective-permute-start(bf16[3,6,128,128]{3,2,1,0:T(8,128)(2,1)S(1)} %pad_maximum_fusion.1), channel_id=1, source_target_pairs={{1,0},{2,1},{3,2},{5,4},{6,5},{7,6},{9,8},{10,9},{11,10},{13,12},{... | collective-permute-start | bytes 1769480 | tf_op jit(solution)/shard_map/ppermute | solution.py:371
  177.0 8.3 %collective-permute-start.6 = (f32[8,16,128]{2,1,0:T(8,128)S(1)}, f32[8,16,128]{2,1,0:T(8,128)S(1)}, u32[]{:S(2)}, u32[]{:S(2)}) collective-permute-start(f32[8,16,128]{2,1,0:T(8,128)S(1)} %outer.1), channel_id=1, source_target_pairs={{0,0},{4,4},{8,8},{12,12},{16,16},{20,20},{24,24},{28,28},{32,32},... | collective-permute-start | bytes 196616 | tf_op jit(solution)/shard_map/ppermute | solution.py:386
